TPU v7x, 512 devices: a whole 4x8x8 slice. The times are simulated.
512 devices in a mesh: row: 64 (over z, y_hi, core), col: 8 (over y_lo, x).
Axes of the slice: x: 4, y: 8 (y_hi: 4, y_lo: 2; y = y_hi * 2 + y_lo), z: 8, core: 2. Of those that a mesh axis runs over, the one named last changes fastest.
Arguments:
- left_projection: bfloat16 [128, 512, 32], P('col', 'row'), may hold values from -6 to 6
- right_projection: bfloat16 [128, 512, 32], P('row', 'col'), may hold values from -6 to 6
- output_weight: bfloat16 [1024, 128], replicated, may hold values from -0.1875 to 0.1875
- pair_update_gradient: bfloat16 [512, 512, 128], P('row', 'col'), may hold values from -6 to 6
- alignment_mask: int32 [128, 512], replicated, may hold values from 0 to 1, as said below
Outputs:
- first_factor_derivative: bfloat16 [128, 512, 32], P('col', 'row')
- grad_right: bfloat16 [128, 512, 32], P('row', 'col')
- grad_wout: float32 [1024, 128], replicated
- grad_bias: float32 [128], replicated
Inputs may be any that keep to these rules, and one draw needn't show every extreme that they name: `alignment_mask`: the last residues of the crop, from 1 to 4 of them, are 0 in every 128 row.
All inputs are finite; a program needn't handle non-finite values.
Results may differ from a plain program's by a relative error of at most 0.0058.
Values may be sent and summed in bfloat16 or wider, within the bound.
No kernel may reach another device: no remote copies, remote signals or barrier semaphores. Data moves between devices by JAX's collectives and lax.ppermute only.
A program may use at most 64 MiB of HBM per device.

v0:
```python
import jax
import jax.numpy as jnp
from jax import lax
from jax.sharding import PartitionSpec as P


def per_device(
    left_projection, right_projection, output_weight, pair_update_gradient, alignment_mask
):
    block_row_span, block_column_span, pair_width = pair_update_gradient.shape
    channel_total = left_projection.shape[2]
    alignment_row_total = alignment_mask.shape[0]
    row_start = lax.axis_index("row") * block_row_span
    column_start = lax.axis_index("col") * block_column_span
    mask_row_view = lax.dynamic_slice_in_dim(alignment_mask, row_start, block_row_span, 1).astype(
        jnp.bfloat16
    )
    mask_column_view = lax.dynamic_slice_in_dim(
        alignment_mask, column_start, block_column_span, 1
    ).astype(jnp.bfloat16)
    counts = jnp.dot(mask_row_view.T, mask_column_view, preferred_element_type=jnp.float32)
    scaled_f = pair_update_gradient.astype(jnp.float32) / jnp.maximum(counts, 1.0)[:, :, None]
    bias_sum = jnp.sum(scaled_f, axis=(0, 1))
    scaled = scaled_f.astype(jnp.bfloat16)
    left_full = lax.all_gather(left_projection, "col", axis=0, tiled=True)
    right_full = lax.all_gather(right_projection, "row", axis=0, tiled=True)
    masked_left_rows = left_full * mask_row_view[:, :, None]
    right_masked = right_full * mask_column_view[:, :, None]
    rows_per_block = 8
    number_of_blocks = block_row_span // rows_per_block
    pair_blocks = scaled.reshape(number_of_blocks, rows_per_block * block_column_span, pair_width)
    left_row_blocks = masked_left_rows.reshape(
        alignment_row_total, number_of_blocks, rows_per_block, channel_total
    ).transpose(1, 0, 2, 3)

    def block_step(totals, pieces):
        weight_sum, right_sum = totals
        pair_flat, left_block = pieces
        grad_outer = jnp.einsum(
            "pk,ok->po", pair_flat, output_weight, preferred_element_type=jnp.float32
        ).astype(jnp.bfloat16)
        grad_outer = grad_outer.reshape(
            rows_per_block, block_column_span, channel_total, channel_total
        )
        outer_tile = jnp.einsum(
            "sic,sjd->ijcd", left_block, right_masked, preferred_element_type=jnp.float32
        ).astype(jnp.bfloat16)
        outer_flat = outer_tile.reshape(
            rows_per_block * block_column_span, channel_total * channel_total
        )
        weight_sum = weight_sum + jnp.einsum(
            "po,pk->ok", outer_flat, pair_flat, preferred_element_type=jnp.float32
        )
        left_grad = jnp.einsum(
            "ijcd,sjd->sic", grad_outer, right_masked, preferred_element_type=jnp.float32
        )
        right_sum = right_sum + jnp.einsum(
            "ijcd,sic->sjd", grad_outer, left_block, preferred_element_type=jnp.float32
        )
        return ((weight_sum, right_sum), left_grad)

    starting_carry = (
        jnp.zeros((channel_total * channel_total, pair_width), jnp.float32),
        jnp.zeros((alignment_row_total, block_column_span, channel_total), jnp.float32),
    )
    totals, first_factor_portions = lax.scan(
        block_step, starting_carry, (pair_blocks, left_row_blocks)
    )
    weight_sum, right_sum = totals
    first_factor_summands = first_factor_portions.transpose(1, 0, 2, 3).reshape(
        alignment_row_total, block_row_span, channel_total
    )
    first_factor_reduced = lax.psum_scatter(
        first_factor_summands, "col", scatter_dimension=0, tiled=True
    )
    left_share = first_factor_reduced.shape[0]
    left_mask = lax.dynamic_slice_in_dim(
        mask_row_view, lax.axis_index("col") * left_share, left_share, 0
    )
    first_factor_derivative = (first_factor_reduced * left_mask[:, :, None]).astype(jnp.bfloat16)
    right_summed = lax.psum_scatter(right_sum, "row", scatter_dimension=0, tiled=True)
    right_share = right_summed.shape[0]
    right_mask = lax.dynamic_slice_in_dim(
        mask_column_view, lax.axis_index("row") * right_share, right_share, 0
    )
    grad_right = (right_summed * right_mask[:, :, None]).astype(jnp.bfloat16)
    grad_wout, grad_bias = lax.psum((weight_sum, bias_sum), ("row", "col"))
    return (first_factor_derivative, grad_right, grad_wout, grad_bias)


def solution(mesh):
    return jax.shard_map(
        per_device,
        mesh=mesh,
        in_specs=(P("col", "row", None), P("row", "col", None), P(), P("row", "col", None), P()),
        out_specs=(P("col", "row", None), P("row", "col", None), P(), P()),
        check_vma=False,
    )
```

profile of v0, /device:TPU:1, one launch (start us, length us, event | category | flops | bytes accessed | tf_op | source)
XLA Modules:
  0.0 444.6 jit_solution(8002552018253836575)
XLA Ops:
  8.1 1.0 dynamic-slice_convert_fusion
  9.1 0.9 constant_dynamic-slice_fusion.1
  10.3 1.6 fusion.11
  12.3 0.5 copy.43
  12.9 1.1 reshape.28
  14.0 98.9 %all_gather.6 = bf16[128,64,32]{1,2,0:T(8,128)(2,1)} all-gather(bf16[2,64,32]{1,2,0:T(8,128)(2,1)} %param.6), channel_id=1, replica_groups=mesh['row'=64,'col'=8] {'row'}, dimensions={0}, use_global_device_ids=true | all-gather | bytes 532480 | tf_op jit(solution)/shard_map/all_gather | solution.py:26
  112.8 2.8 copy.41
  115.7 4.8 %copy.52 = bf16[8,64,32,32]{2,3,1,0:T(8,128)(2,1)} copy(bf16[8,64,32,32]{1,0,3,2:T(8,128)(2,1)S(1)} %reshape.28) | data formatting | bytes 2097152 | tf_op jit(solution)/shard_map/while/body/eval_jaxpr/reshape | solution.py:42
  120.5 3.7 convolution_bitcast_fusion
  124.3 23.7 %all_gather.7 = bf16[128,8,32]{2,1,0:T(8,128)(2,1)S(1)} all-gather(bf16[16,8,32]{2,1,0:T(8,128)(2,1)S(1)} %copy-done.5), channel_id=1, replica_groups=mesh['row'=64,'col'=8] {'col'}, dimensions={0}, use_global_device_ids=true | all-gather | bytes 73728 | tf_op jit(solution)/shard_map/all_gather | solution.py:25
  148.2 2.4 fusion.2
  150.6 4.0 copy.48
  154.9 3.2 convert_bitcast_fusion
  158.1 7.8 %copy.49 = bf16[8,64,32,32]{1,0,3,2:T(8,128)(2,1)S(1)} copy(bf16[8,64,32,32]{2,3,0,1:T(8,128)(2,1)} %convert_bitcast_fusion) | data formatting | bytes 2097152 | tf_op jit(solution)/shard_map/while/body/eval_jaxpr/convert_element_type | solution.py:47
  166.0 1.3 reshape.29
  167.2 1.2 fusion.20
  168.5 0.7 fusion.19
  169.3 100.3 %psum.15 = f32[128]{0:T(128)} all-reduce(f32[128]{0:T(128)S(1)} %copy-done.6), channel_id=1, replica_groups=mesh['row'=64,'col'=8] {'row','col'}, use_global_device_ids=true, to_apply=%region_4.5 | all-reduce | flops 128 | bytes 1024 | tf_op jit(solution)/shard_map/psum | solution.py:87
  269.5 0.9 multiply_convert_fusion
  270.5 0.6 copy.50
  271.1 37.8 %reduce-scatter.5.cloned.1.call-done = f32[2,64,32]{1,2,0:T(8,128)} async-done(((f32[128,64,32]{1,2,0:T(8,128)}), f32[2,64,32]{1,2,0:T(8,128)}) %reduce-scatter.5.cloned.1.call-update) | async-done | bytes 16400 | tf_op jit(solution)/shard_map/reduce_scatter | solution.py:81
  308.9 1.4 multiply_convert_fusion.1
  310.3 125.0 %all-reduce.2.cloned.1.call-done = f32[1024,128]{1,0:T(8,128)} async-done(((f32[1024,128]{1,0:T(8,128)}), f32[1024,128]{1,0:T(8,128)}) %all-reduce.2.cloned.1.call-update) | async-done | bytes 524304 | tf_op jit(solution)/shard_map/psum | solution.py:87
  435.2 1.9 copy.66
  (28 shorter events, 1.4 us)
Async XLA Ops:
  8.0 3.9 copy-start
  8.0 261.5 %reduce-scatter.3.cloned.1.call-start = ((), (), s32[]{:S(2)}) async-start(), calls=%async_computation.2 | async-start | bytes 589824 | tf_op jit(solution)/shard_map/reduce_scatter | solution.py:73
  9.0 2.8 copy-start.1
  10.1 1.7 copy-start.2
  120.5 3.8 copy-start.5
  120.5 27.8 %copy-start.3 = (bf16[128,8]{0,1:T(8,128)(2,1)S(1)}, bf16[128,8]{0,1:T(8,128)(2,1)}, u32[]{:S(2)}) copy-start(bf16[128,8]{0,1:T(8,128)(2,1)} %copy-done.2) | copy-start | bytes 6148
  124.2 184.7 %reduce-scatter.5.cloned.1.call-start = ((), (), s32[]{:S(2)}) async-start(), calls=%async_computation.3 | async-start | bytes 2129920 | tf_op jit(solution)/shard_map/reduce_scatter | solution.py:81
  154.7 280.6 %all-reduce.2.cloned.1.call-start = ((), (), s32[]{:S(2)}) async-start(), calls=%async_computation.4 | async-start | bytes 1048576 | tf_op jit(solution)/shard_map/psum | solution.py:87
  165.9 3.2 copy-start.4
  165.9 3.3 copy-start.6
Sparse Core Ops, SparseCore 0:
  124.3 28.9 reduce-scatter.2
  158.7 150.1 reduce-scatter.4
Sparse Core Ops, SparseCore 1:
  168.6 266.6 all-reduce.1
where the time goes:
time: 445 us
  blocking collectives  223 us (50%)
  waiting for transfers between devices  163 us (37%)
  local copies, waits for them, and re-layouts  26.1 us (6%)
  between operations  15.6 us (4%)
  matrix products  11.2 us (3%)
  other arithmetic  5.59 us (1%)
    psum x1, waiting for transfers between devices, per_device(): grad_wout, grad_bias = lax.psum((weight_sum, bias_sum), ('row', 'col'))  125 us
    psum x1, blocking collectives, per_device(): grad_wout, grad_bias = lax.psum((weight_sum, bias_sum), ('row', 'col'))  100 us
    all_gather x1, blocking collectives, per_device(): right_full = lax.all_gather(right_projection, 'row', axis=0, tiled=True)  98.9 us
    reduce_scatter x1, waiting for transfers between devices, per_device(): lax.psum_scatter(right_sum, 'row', scatter_dimension=0, tiled=True)  37.8 us
    all_gather x1, blocking collectives, per_device(): left_full = lax.all_gather(left_projection, 'col', axis=0, tiled=True)  23.7 us
  transfers between devices with their start and end apart: 3, of which 2 were waited for; matrix products, arithmetic and copies ran while one was open for 5% of the time, Pallas kernels for 0%

commit v1 on v0

v1 whole, which is shorter than its diff:
```python
import jax
import jax.numpy as jnp
from jax import lax
from jax.experimental import pallas as pl
from jax.experimental.pallas import tpu as pltpu
from jax.sharding import Mesh
from jax.sharding import PartitionSpec as P

SHAPE = (8, 4, 2, 2, 4)
NAMES = ("z", "yh", "core", "yl", "x")
ROW = ("z", "yh", "core")
ZY = ("z", "yh")
COL = ("yl", "x")
CHIP_COL = ("core", "yl", "x")
C = 32
K = 128
S = 128
TI, TJ = 16, 32
F32, BF16 = jnp.float32, jnp.bfloat16
VMEM = pl.BlockSpec(memory_space=pltpu.VMEM)


def dot(a, b, ca, cb):
    return lax.dot_general(a, b, (((ca,), (cb,)), ((), ())), preferred_element_type=F32)


def scale_kernel(pair_ref, mi_ref, mj_ref, w_ref, s_ref, bias_ref, g_ref):
    live = mi_ref[...][:, None, :] * mj_ref[...][None, :, :]
    live = live.reshape(TI * TJ, S).astype(BF16)
    counts = dot(live, jnp.ones((S, K), BF16), 1, 0)
    scaled = pair_ref[...].reshape(TI * TJ, K).astype(F32) / jnp.maximum(counts, 1.0)
    total = jnp.sum(scaled, axis=0, keepdims=True)
    high = total.astype(BF16).astype(F32)
    row = lax.broadcasted_iota(jnp.int32, (8, K), 0)
    bias_ref[...] = jnp.where(row == 0, high, jnp.where(row == 1, total - high, 0.0)).astype(BF16)
    scaled = scaled.astype(BF16)
    s_ref[...] = scaled
    for g in range(C // 4):
        part = dot(w_ref[g * 4 * C : (g + 1) * 4 * C, :], scaled, 1, 1).astype(BF16)
        for i in range(TI):
            g_ref[i * C : (i + 1) * C, g * K : (g + 1) * K] = jnp.concatenate(
                [part[e * C : (e + 1) * C, i * TJ : (i + 1) * TJ] for e in range(4)], axis=1
            )


def main_kernel(l_ref, r_ref, s_ref, g_ref, left_ref, right_ref, wout_ref, o_ref):
    left = jnp.concatenate([l_ref[0], l_ref[1]], axis=1)
    right = r_ref[...]
    o_ref[...] = dot(left, right, 0, 0).astype(BF16)
    pairs = s_ref[...]
    for g in range(C // 4):
        rows = []
        for e in range(4):
            at = g * K + e * TJ
            rows.append(
                jnp.concatenate(
                    [o_ref[i * C : (i + 1) * C, at : at + TJ] for i in range(TI)], axis=1
                )
            )
        outer = jnp.concatenate(rows, axis=0)
        wout_ref[g * 4 * C : (g + 1) * 4 * C, :] = dot(outer, pairs, 1, 0).astype(BF16)
    grad = g_ref[...]
    right_ref[...] = dot(left, grad, 1, 0).astype(BF16)
    left_ref[...] = dot(right, grad, 1, 1).astype(BF16)


def per_device(left, right, weight, pair, mask):
    row_at = lax.axis_index(ROW)
    zy_at = lax.axis_index(ZY)
    col_at = lax.axis_index(COL)
    core_at = lax.axis_index("core")
    pair = lax.all_to_all(pair.reshape(8, 2, TJ, K), "core", 1, 0, tiled=True)
    pair = pair.reshape(2, 8, TJ, K).reshape(TI, TJ, K)
    mask_i = lax.dynamic_slice_in_dim(mask, zy_at * TI, TI, 1).T.astype(F32)
    mask_j = lax.dynamic_slice_in_dim(mask, col_at * 64 + core_at * TJ, TJ, 1).T.astype(F32)
    weight = weight.reshape(C, C, K).transpose(1, 0, 2).reshape(C * C, K)
    right_mask = lax.dynamic_slice(mask, (row_at * 2, col_at * 64), (2, 64)).astype(BF16)
    send = (right * right_mask[:, :, None]).transpose(0, 2, 1).reshape(2, C, 2, TJ)
    send = send.transpose(2, 0, 1, 3).reshape(1, 2, 2, C * TJ)
    send = jnp.broadcast_to(send, (32, 2, 2, C * TJ)).reshape(64, 2, C * TJ)
    right_all = lax.all_to_all(send, ROW, 0, 0, tiled=True).reshape(S, C * TJ)
    left_mask = lax.dynamic_slice(mask, (col_at * 16, row_at * 8), (16, 8)).astype(BF16)
    send = (left * left_mask[:, :, None]).reshape(1, 16, 8 * C)
    send = jnp.broadcast_to(send, (16, 16, 8 * C))
    left_all = lax.all_to_all(send, CHIP_COL, 0, 0, tiled=True).reshape(2, S, 8 * C)

    scaled, bias, grad = pl.pallas_call(
        scale_kernel,
        out_shape=(
            jax.ShapeDtypeStruct((TI * TJ, K), BF16),
            jax.ShapeDtypeStruct((8, K), BF16),
            jax.ShapeDtypeStruct((TI * C, C * TJ), BF16),
        ),
        in_specs=[VMEM] * 4,
        out_specs=(VMEM,) * 3,
        compiler_params=pltpu.CompilerParams(vmem_limit_bytes=32 << 20),
        cost_estimate=pl.CostEstimate(flops=150_000_000, bytes_accessed=2_000_000, transcendentals=0),
    )(pair, mask_i, mask_j, weight)
    left_part, right_part, wout_part = pl.pallas_call(
        main_kernel,
        out_shape=(
            jax.ShapeDtypeStruct((S, TI * C), BF16),
            jax.ShapeDtypeStruct((S, C * TJ), BF16),
            jax.ShapeDtypeStruct((C * C, K), BF16),
        ),
        in_specs=[VMEM] * 4,
        out_specs=(VMEM,) * 3,
        scratch_shapes=[pltpu.VMEM((TI * C, C * TJ), BF16)],
        compiler_params=pltpu.CompilerParams(vmem_limit_bytes=32 << 20),
        cost_estimate=pl.CostEstimate(flops=600_000_000, bytes_accessed=3_000_000, transcendentals=0),
    )(left_all, right_all, scaled, grad)

    send = jnp.concatenate(
        [
            right_part.reshape(64, 16, K),
            wout_part.reshape(64, 16, K),
            jnp.broadcast_to(bias[None], (64, 8, K)),
        ],
        axis=1,
    )
    got = lax.all_to_all(send, ROW, 0, 0, tiled=True).astype(F32).reshape(32, 2, 40, K)
    total = jnp.sum(got[:, :, 16:], axis=(0, 1))
    right_sum = jnp.sum(got[:, :, :16], axis=0).reshape(2, 2, C, TJ)
    right_grad = right_sum.transpose(1, 0, 3, 2).reshape(2, 64, C)
    right_grad = (right_grad * right_mask.astype(F32)[:, :, None]).astype(BF16)
    bias_sum = total[16] + total[17]
    high = lax.reduce_precision(bias_sum, 8, 7)
    bias_rows = jnp.concatenate([high[None], (bias_sum - high)[None], jnp.zeros((6, K), F32)])
    left_send = left_part.reshape(8, 16, 2, 8 * C).transpose(2, 0, 1, 3).reshape(16, 32, K)
    rows = jnp.concatenate([total[:16], bias_rows]).astype(BF16)
    send = jnp.concatenate([left_send, jnp.broadcast_to(rows[None], (16, 24, K))], axis=1)
    got = lax.all_to_all(send, CHIP_COL, 0, 0, tiled=True).astype(F32)
    left_grad = jnp.sum(got[:, :32], axis=0).reshape(16, 8, C)
    left_grad = (left_grad * left_mask.astype(F32)[:, :, None]).astype(BF16)
    bias_sum = jnp.sum(got[:, 48:50], axis=(0, 1)) * 0.5
    rows = jnp.sum(got[:, 32:48].reshape(2, 8, 16, K), axis=1).reshape(1, 32, K).astype(BF16)
    wout = lax.all_to_all(jnp.broadcast_to(rows, (32, 32, K)), ZY, 0, 0, tiled=True)
    wout = wout.reshape(C, C, K).transpose(1, 0, 2).reshape(C * C, K).astype(F32)
    return left_grad, right_grad, wout, bias_sum


def solution(mesh):
    parts = Mesh(mesh.devices.reshape(SHAPE), NAMES)
    left_spec, right_spec = P(COL, ROW, None), P(ROW, COL, None)
    return jax.shard_map(
        per_device,
        mesh=parts,
        in_specs=(left_spec, right_spec, P(), P(ROW, COL, None), P()),
        out_specs=(left_spec, right_spec, P(), P()),
        check_vma=False,
    )
```

time: 445 us -> 117 us (0.26)
  blocking collectives: 223 us -> 0 us
  waiting for transfers between devices: 163 us -> 60.3 us
  starting transfers between devices: 0.3 us -> 39.9 us
  local copies, waits for them, and re-layouts: 26.1 us -> 5.31 us
  between operations: 15.6 us -> 0.85 us
  matrix products: 11.2 us -> 0 us
    psum x1 -> x0, waiting for transfers between devices: 125 us -> none  [per_device(): grad_wout, grad_bias = lax.psum((weight_sum, bias_sum), ('row', 'col'))]
    all_gather x2 -> x0, blocking collectives: 123 us -> none  [the longest x1 98.9 us: per_device(): right_full = lax.all_gather(right_projection, 'row', axis=0, tiled=True)]
    psum x1 -> x0, blocking collectives: 100 us -> none  [per_device(): grad_wout, grad_bias = lax.psum((weight_sum, bias_sum), ('row', 'col'))]
    all_to_all x0 -> x6, waiting for transfers between devices: none -> 60.3 us  [the longest x1 22.5 us: per_device(): lax.all_to_all(send, ROW, 0, 0, tiled=True).astype(F32)]
    all_to_all x0 -> x6, starting transfers between devices: none -> 39.9 us  [the longest x1 10.9 us: per_device(): right_all = lax.all_to_all(send, ROW, 0, 0, tiled=True).reshape(S, C * TJ)]
    reduce_scatter x2 -> x0, waiting for transfers between devices: 37.8 us -> none  [the longest x1 37.8 us: per_device(): lax.psum_scatter(right_sum, 'row', scatter_dimension=0, tiled=True)]
    dot_general x6 -> x0, matrix products: 11.2 us -> none  [the longest x1 3.73 us: block_step(): jnp.einsum('ijcd,sjd->sic', grad_outer, right_masked, preferred_element_t...]
    convert_element_type x3 -> x0, local copies, waits for them, and re-layouts: 8.43 us -> none  [the longest x1 7.8 us: block_step(): outer_tile = jnp.einsum('sic,sjd->ijcd', left_block, right_masked, prefer...]
  transfers between devices with their start and end apart: 3 -> 6, of which waited for: 2 -> 5; matrix products, arithmetic and copies ran while one was open for 5% -> 5% of each run, Pallas kernels for 0% -> 1%
where the time goes in v1:
time: 117 us; the launch traced here: 116 us
  waiting for transfers between devices  60.3 us (52%)
  starting transfers between devices  39.9 us (34%)
  other arithmetic  7.07 us (6%)
  local copies, waits for them, and re-layouts  5.31 us (5%)
  Pallas kernels  2.95 us (3%)
    all_to_all x1, waiting for transfers between devices, per_device(): lax.all_to_all(send, ROW, 0, 0, tiled=True).astype(F32)  22.5 us
    all_to_all x1, waiting for transfers between devices, per_device(): right_all = lax.all_to_all(send, ROW, 0, 0, tiled=True).reshape(S, C * TJ)  14.9 us
    all_to_all x1, waiting for transfers between devices, per_device(): lax.all_to_all(jnp.broadcast_to(rows, (32, 32, K)), ZY, 0, 0, tiled=True)  11.7 us
    all_to_all x1, starting transfers between devices, per_device(): right_all = lax.all_to_all(send, ROW, 0, 0, tiled=True).reshape(S, C * TJ)  10.9 us
    all_to_all x1, starting transfers between devices, per_device(): pair = lax.all_to_all(pair.reshape(8, 2, TJ, K), 'core', 1, 0, tiled=True)  10.2 us
    all_to_all x1, waiting for transfers between devices, per_device(): got = lax.all_to_all(send, CHIP_COL, 0, 0, tiled=True).astype(F32)  6.5 us
    all_to_all x1, starting transfers between devices, per_device(): lax.all_to_all(jnp.broadcast_to(rows, (32, 32, K)), ZY, 0, 0, tiled=True)  5.07 us
    all_to_all x1, starting transfers between devices, per_device(): lax.all_to_all(send, CHIP_COL, 0, 0, tiled=True).reshape(2, S, 8 * C)  4.73 us
  transfers between devices with their start and end apart: 6, of which 5 were waited for; matrix products, arithmetic and copies ran while one was open for 5% of the time, Pallas kernels for 1%

profile of v1, /device:TPU:1, one launch (start us, length us, event | category | flops | bytes accessed | tf_op | source)
XLA Modules:
  0.0 116.3 jit_solution(16889798643423166881)
XLA Ops:
  0.7 1.6 %copy.34 = bf16[8,2,32,128]{3,2,0,1:T(8,128)(2,1)} copy(bf16[8,2,32,128]{3,2,1,0:T(8,128)(2,1)} %bitcast.50) | data formatting | bytes 262144 | tf_op jit(solution)/shard_map/reshape | solution.py:72
  2.3 10.2 %all-to-all-start.2 = ((bf16[8,2,32,128]{3,2,0,1:T(8,128)(2,1)}), bf16[8,2,32,128]{3,2,0,1:T(8,128)(2,1)S(1)}, u32[]{:S(2)}, u32[]{:S(2)}) async-start(bf16[8,2,32,128]{3,2,0,1:T(8,128)(2,1)} %copy.34), calls=%async_computation.2 | async-start | bytes 262144 | tf_op jit(solution)/shard_map/all_to_all | solution.py:72
  12.5 0.8 fusion.1
  13.3 0.7 multiply_bitcast_fusion
  14.2 0.8 fusion.2
  15.0 0.8 broadcast_in_dim.19
  15.8 10.9 %all-to-all-start.1 = ((bf16[64,2,1024]{2,1,0:T(2,128)(2,1)}), bf16[64,2,1024]{2,1,0:T(2,128)(2,1)S(1)}, u32[]{:S(2)}, u32[]{:S(2)}) async-start(bf16[64,2,1024]{2,1,0:T(2,128)(2,1)} %bitcast.3), calls=%async_computation.1 | async-start | bytes 524288 | tf_op jit(solution)/shard_map/all_to_all | solution.py:81
  27.1 14.9 %all-to-all-done.1 = bf16[64,2,1024]{2,1,0:T(2,128)(2,1)S(1)} async-done(((bf16[64,2,1024]{2,1,0:T(2,128)(2,1)}), bf16[64,2,1024]{2,1,0:T(2,128)(2,1)S(1)}, u32[]{:S(2)}, u32[]{:S(2)}) %all-to-all-start.1) | async-done | bytes 262176 | tf_op jit(solution)/shard_map/all_to_all | solution.py:81
  42.0 0.7 broadcast_in_dim.17
  42.6 4.7 %all-to-all-start = ((bf16[16,16,256]{2,1,0:T(8,128)(2,1)}), bf16[16,16,256]{2,1,0:T(8,128)(2,1)S(1)}, u32[]{:S(2)}, u32[]{:S(2)}) async-start(bf16[16,16,256]{2,1,0:T(8,128)(2,1)} %broadcast_in_dim.17), calls=%async_computation | async-start | bytes 262144 | tf_op jit(solution)/shard_map/all_to_all | solution.py:85
  47.7 1.2 %shard_map.84 = (bf16[512,128]{1,0:T(8,128)(2,1)S(1)}, bf16[8,128]{1,0:T(8,128)(2,1)S(1)}, bf16[512,1024]{1,0:T(8,128)(2,1)S(1)}) custom-call(bf16[16,32,128]{2,1,0:T(8,128)(2,1)S(1)} %bitcast.43, f32[16,128]{1,0:T(8,128)S(1)} %convert_bitcast_fusion.1.mi_ref, f32[32,128]{1,0:T(8,128)S(1)} %convert_bitcast_fusion.mj_ref, bf16[1024,128]{1,0:T(8,128)(2,1)S(1)} %bitcast.42), custom_call_target="tpu_custom_call" | custom-call | flops 150000000 | bytes 2000000 | tf_op jit(solution)/shard_map/pallas_call | solution.py:87
  49.0 4.7 %all-to-all-done = bf16[16,16,256]{2,1,0:T(8,128)(2,1)S(1)} async-done(((bf16[16,16,256]{2,1,0:T(8,128)(2,1)}), bf16[16,16,256]{2,1,0:T(8,128)(2,1)S(1)}, u32[]{:S(2)}, u32[]{:S(2)}) %all-to-all-start) | async-done | bytes 131104 | tf_op jit(solution)/shard_map/all_to_all | solution.py:85
  53.7 1.7 %shard_map.85 = (bf16[128,512]{1,0:T(8,128)(2,1)S(1)}, bf16[128,1024]{1,0:T(8,128)(2,1)S(1)}, bf16[1024,128]{1,0:T(8,128)(2,1)S(1)}) custom-call(bf16[2,128,256]{2,1,0:T(8,128)(2,1)S(1)} %bitcast.44, bf16[128,1024]{1,0:T(8,128)(2,1)S(1)} %reshape.110.r_ref, bf16[512,128]{1,0:T(8,128)(2,1)S(1)} %get-tuple-element.10.s_ref, ...), custom_call_target="tpu_custom_call" | custom-call | flops 600000000 | bytes 3000000 | tf_op jit(solution)/shard_map/pallas_call | solution.py:99
  55.6 0.9 pad_maximum_fusion
  56.5 4.5 %all-to-all-start.3 = ((bf16[64,40,128]{2,1,0:T(8,128)(2,1)}), bf16[64,40,128]{2,1,0:T(8,128)(2,1)S(1)}, u32[]{:S(2)}, u32[]{:S(2)}) async-start(bf16[64,40,128]{2,1,0:T(8,128)(2,1)} %pad_maximum_fusion), calls=%async_computation.3 | async-start | bytes 1310720 | tf_op jit(solution)/shard_map/all_to_all | solution.py:121
  61.2 22.5 %all-to-all-done.3 = bf16[64,40,128]{2,1,0:T(8,128)(2,1)S(1)} async-done(((bf16[64,40,128]{2,1,0:T(8,128)(2,1)}), bf16[64,40,128]{2,1,0:T(8,128)(2,1)S(1)}, u32[]{:S(2)}, u32[]{:S(2)}) %all-to-all-start.3) | async-done | bytes 655392 | tf_op jit(solution)/shard_map/all_to_all | solution.py:121
  84.0 0.7 pad_maximum_fusion.1
  84.7 4.4 %all-to-all-start.4 = ((bf16[16,56,128]{2,1,0:T(8,128)(2,1)}), bf16[16,56,128]{2,1,0:T(8,128)(2,1)S(1)}, u32[]{:S(2)}, u32[]{:S(2)}) async-start(bf16[16,56,128]{2,1,0:T(8,128)(2,1)} %pad_maximum_fusion.1), calls=%async_computation.4 | async-start | bytes 458752 | tf_op jit(solution)/shard_map/all_to_all | solution.py:132
  90.0 6.5 %all-to-all-done.4 = bf16[16,56,128]{2,1,0:T(8,128)(2,1)S(1)} async-done(((bf16[16,56,128]{2,1,0:T(8,128)(2,1)}), bf16[16,56,128]{2,1,0:T(8,128)(2,1)S(1)}, u32[]{:S(2)}, u32[]{:S(2)}) %all-to-all-start.4) | async-done | bytes 229408 | tf_op jit(solution)/shard_map/all_to_all | solution.py:132
  96.6 0.7 broadcast_in_dim.23
  97.3 5.1 %all-to-all-start.5 = ((bf16[32,32,128]{2,1,0:T(8,128)(2,1)}), bf16[32,32,128]{2,1,0:T(8,128)(2,1)S(1)}, u32[]{:S(2)}, u32[]{:S(2)}) async-start(bf16[32,32,128]{2,1,0:T(8,128)(2,1)} %broadcast_in_dim.23), calls=%async_computation.5 | async-start | bytes 524288 | tf_op jit(solution)/shard_map/all_to_all | solution.py:137
  103.0 0.7 multiply_convert_fusion
  103.7 11.7 %all-to-all-done.5 = bf16[32,32,128]{2,1,0:T(8,128)(2,1)S(1)} async-done(((bf16[32,32,128]{2,1,0:T(8,128)(2,1)}), bf16[32,32,128]{2,1,0:T(8,128)(2,1)S(1)}, u32[]{:S(2)}, u32[]{:S(2)}) %all-to-all-start.5) | async-done | bytes 262176 | tf_op jit(solution)/shard_map/all_to_all | solution.py:137
  115.4 0.9 copy_convert_fusion
  (44 shorter events, 3.1 us)
Async XLA Ops:
  0.6 26.3 %copy-start.1 = (s32[128,512]{1,0:T(8,128)S(1)}, s32[128,512]{1,0:T(8,128)}, u32[]{:S(2)}) copy-start(s32[128,512]{1,0:T(8,128)} %param.9) | copy-start | bytes 786436
  0.6 26.1 %copy-start.2 = (bf16[16,8,32]{2,1,0:T(8,128)(2,1)S(1)}, bf16[16,8,32]{2,1,0:T(8,128)(2,1)}, u32[]{:S(2)}) copy-start(bf16[16,8,32]{2,1,0:T(8,128)(2,1)} %param.5) | copy-start | bytes 24580
  0.7 46.9 %copy-start = (bf16[1024,128]{1,0:T(8,128)(2,1)S(1)}, bf16[1024,128]{1,0:T(8,128)(2,1)}, u32[]{:S(2)}) copy-start(bf16[1024,128]{1,0:T(8,128)(2,1)} %param.7) | copy-start | bytes 786436
  2.3 12.7 %all-to-all-start.2 = ((bf16[8,2,32,128]{3,2,0,1:T(8,128)(2,1)}), bf16[8,2,32,128]{3,2,0,1:T(8,128)(2,1)S(1)}, u32[]{:S(2)}, u32[]{:S(2)}) async-start(bf16[8,2,32,128]{3,2,0,1:T(8,128)(2,1)} %copy.34), calls=%async_computation.2 | async-start | bytes 262144 | tf_op jit(solution)/shard_map/all_to_all | solution.py:72
  15.8 26.1 %all-to-all-start.1 = ((bf16[64,2,1024]{2,1,0:T(2,128)(2,1)}), bf16[64,2,1024]{2,1,0:T(2,128)(2,1)S(1)}, u32[]{:S(2)}, u32[]{:S(2)}) async-start(bf16[64,2,1024]{2,1,0:T(2,128)(2,1)} %bitcast.3), calls=%async_computation.1 | async-start | bytes 524288 | tf_op jit(solution)/shard_map/all_to_all | solution.py:81
  42.6 11.1 %all-to-all-start = ((bf16[16,16,256]{2,1,0:T(8,128)(2,1)}), bf16[16,16,256]{2,1,0:T(8,128)(2,1)S(1)}, u32[]{:S(2)}, u32[]{:S(2)}) async-start(bf16[16,16,256]{2,1,0:T(8,128)(2,1)} %broadcast_in_dim.17), calls=%async_computation | async-start | bytes 262144 | tf_op jit(solution)/shard_map/all_to_all | solution.py:85
  56.5 27.2 %all-to-all-start.3 = ((bf16[64,40,128]{2,1,0:T(8,128)(2,1)}), bf16[64,40,128]{2,1,0:T(8,128)(2,1)S(1)}, u32[]{:S(2)}, u32[]{:S(2)}) async-start(bf16[64,40,128]{2,1,0:T(8,128)(2,1)} %pad_maximum_fusion), calls=%async_computation.3 | async-start | bytes 1310720 | tf_op jit(solution)/shard_map/all_to_all | solution.py:121
  84.7 11.8 %all-to-all-start.4 = ((bf16[16,56,128]{2,1,0:T(8,128)(2,1)}), bf16[16,56,128]{2,1,0:T(8,128)(2,1)S(1)}, u32[]{:S(2)}, u32[]{:S(2)}) async-start(bf16[16,56,128]{2,1,0:T(8,128)(2,1)} %pad_maximum_fusion.1), calls=%async_computation.4 | async-start | bytes 458752 | tf_op jit(solution)/shard_map/all_to_all | solution.py:132
  97.3 18.1 %all-to-all-start.5 = ((bf16[32,32,128]{2,1,0:T(8,128)(2,1)}), bf16[32,32,128]{2,1,0:T(8,128)(2,1)S(1)}, u32[]{:S(2)}, u32[]{:S(2)}) async-start(bf16[32,32,128]{2,1,0:T(8,128)(2,1)} %broadcast_in_dim.23), calls=%async_computation.5 | async-start | bytes 524288 | tf_op jit(solution)/shard_map/all_to_all | solution.py:137

commit v2 on v1

v2 whole, which is shorter than its diff:
```python
import jax
import jax.numpy as jnp
from jax import lax
from jax.experimental import pallas as pl
from jax.experimental.pallas import tpu as pltpu
from jax.sharding import Mesh
from jax.sharding import PartitionSpec as P

SHAPE = (4, 2, 4, 2, 2, 4)
NAMES = ("zq", "zb", "yh", "core", "yl", "x")
ROW = ("zq", "zb", "yh", "core")
ZY = ("zq", "zb", "yh")
COL = ("yl", "x")
NEAR = ("zb", "core", "yl", "x")
FAR = ("zq", "yh")
C = 32
K = 128
S = 128
TI, TJ = 16, 32
F32, BF16 = jnp.float32, jnp.bfloat16
VMEM = pl.BlockSpec(memory_space=pltpu.VMEM)
SMEM = pl.BlockSpec(memory_space=pltpu.SMEM)


def dot(a, b, ca, cb):
    return lax.dot_general(a, b, (((ca,), (cb,)), ((), ())), preferred_element_type=F32)


def scale_kernel(
    at_ref, keep_ref, take_ref, m_ref, mi_ref, mj_ref, w_ref, l_in,
    s_ref, bias_ref, g_ref, l_ref, rkeep_ref, rgive_ref, right_ref,
):
    keep, take = keep_ref[...], take_ref[...]
    first = at_ref[0] == 0
    pair = jnp.concatenate([jnp.where(first, keep, take), jnp.where(first, take, keep)])
    live = mi_ref[...][:, None, :] * mj_ref[...][None, :, :]
    live = live.reshape(TI * TJ, S).astype(BF16)
    counts = dot(live, jnp.ones((S, K), BF16), 1, 0)
    scaled = pair.reshape(TI * TJ, K).astype(F32) / jnp.maximum(counts, 1.0)
    total = jnp.sum(scaled, axis=0, keepdims=True)
    high = total.astype(BF16).astype(F32)
    row = lax.broadcasted_iota(jnp.int32, (8, K), 0)
    bias_ref[...] = jnp.where(row == 0, high, jnp.where(row == 1, total - high, 0.0)).astype(BF16)
    scaled = scaled.astype(BF16)
    s_ref[...] = scaled
    for g in range(C // 4):
        part = dot(w_ref[g * 4 * C : (g + 1) * 4 * C, :], scaled, 1, 1).astype(BF16)
        for i in range(TI):
            g_ref[i * C : (i + 1) * C, g * K : (g + 1) * K] = jnp.concatenate(
                [part[e * C : (e + 1) * C, i * TJ : (i + 1) * TJ] for e in range(4)], axis=1
            )
    lane = lax.broadcasted_iota(jnp.int32, (TI, TI * C), 1) // C
    spread = (lane == lax.broadcasted_iota(jnp.int32, (TI, TI * C), 0)).astype(BF16)
    live = dot(m_ref[...], spread, 1, 0).astype(BF16)
    for core in range(2):
        lanes = slice(core * 8 * C, (core + 1) * 8 * C)
        for col in range(8):
            rows = slice(col * 16, (col + 1) * 16)
            l_ref[rows, lanes] = l_in[core * 8 + col] * live[rows, lanes]
    right_ref[...] = dot(l_ref[...], g_ref[...], 1, 0).astype(BF16)
    zb = at_ref[1]
    for zq in range(4):
        at = zq * 32 + zb * 16
        rkeep_ref[zq] = right_ref[pl.ds(pl.multiple_of(at, 16), 16), :]
        at = zq * 32 + (1 - zb) * 16
        rgive_ref[zq] = right_ref[pl.ds(pl.multiple_of(at, 16), 16), :]


def main_kernel(
    l_ref, r_ref, m_ref, s_ref, g_ref, rkeep_ref, rtake_ref, left_ref, wout_ref, rsum_ref, o_ref, w_ref
):
    rsum_ref[...] = (rkeep_ref[...].astype(F32) + rtake_ref[...].astype(F32)).astype(BF16)
    right = r_ref[...] * jnp.concatenate([m_ref[...]] * C, axis=1)
    o_ref[...] = dot(l_ref[...], right, 0, 0).astype(BF16)
    pairs = s_ref[...]
    for g in range(C // 4):
        rows = []
        for e in range(4):
            at = g * K + e * TJ
            rows.append(
                jnp.concatenate(
                    [o_ref[i * C : (i + 1) * C, at : at + TJ] for i in range(TI)], axis=1
                )
            )
        outer = jnp.concatenate(rows, axis=0)
        w_ref[g * 4 * C : (g + 1) * 4 * C, :] = dot(outer, pairs, 1, 0)
    for c in range(C):
        wout_ref[c * C : (c + 1) * C, :] = w_ref[pl.ds(c, C, stride=C), :].astype(BF16)
    left_ref[...] = dot(right, g_ref[...], 1, 1).astype(BF16)


def turn(x, axis, by):
    n = SHAPE[NAMES.index(axis)]
    return lax.ppermute(x, axis, [(i, (i + by) % n) for i in range(n)])


def per_device(left, right, weight, pair, mask):
    row_at = lax.axis_index(ROW)
    zy_at = lax.axis_index(ZY)
    col_at = lax.axis_index(COL)
    core_at = lax.axis_index("core")
    zb_at = lax.axis_index("zb")
    send = jnp.broadcast_to(left.reshape(1, 16, 8 * C), (16, 16, 8 * C))
    left_all = lax.all_to_all(send, ("core",) + COL, 0, 0, tiled=True)
    send = right.transpose(0, 2, 1).reshape(2, C, 2, TJ)
    send = send.transpose(2, 0, 1, 3).reshape(1, 2, 2, C * TJ)
    send = jnp.broadcast_to(send, (32, 2, 2, C * TJ)).reshape(64, 2, C * TJ)
    right_all = lax.all_to_all(send, ROW, 0, 0, tiled=True).reshape(S, C * TJ)
    keep = lax.dynamic_slice_in_dim(pair, core_at * TJ, TJ, 1)
    give = lax.dynamic_slice_in_dim(pair, (1 - core_at) * TJ, TJ, 1)
    take = turn(give, "core", 1)
    mask_i = lax.dynamic_slice_in_dim(mask, zy_at * TI, TI, 1)
    mask_j = lax.dynamic_slice_in_dim(mask, col_at * 64 + core_at * TJ, TJ, 1)
    weight = weight.reshape(C, C, K).transpose(1, 0, 2).reshape(C * C, K)
    at = jnp.stack([core_at, zb_at]).astype(jnp.int32)

    scaled, bias, grad, left_all, right_keep, right_give = pl.pallas_call(
        scale_kernel,
        out_shape=(
            jax.ShapeDtypeStruct((TI * TJ, K), BF16),
            jax.ShapeDtypeStruct((8, K), BF16),
            jax.ShapeDtypeStruct((TI * C, C * TJ), BF16),
            jax.ShapeDtypeStruct((S, TI * C), BF16),
            jax.ShapeDtypeStruct((4, 16, C * TJ), BF16),
            jax.ShapeDtypeStruct((4, 16, C * TJ), BF16),
        ),
        in_specs=[SMEM] + [VMEM] * 7,
        out_specs=(VMEM,) * 6,
        scratch_shapes=[pltpu.VMEM((S, C * TJ), BF16)],
        compiler_params=pltpu.CompilerParams(vmem_limit_bytes=32 << 20),
        cost_estimate=pl.CostEstimate(flops=300_000_000, bytes_accessed=3_000_000, transcendentals=0),
    )(
        at, keep, take, mask_i.astype(BF16), mask_i.T.astype(F32), mask_j.T.astype(F32), weight, left_all
    )
    left_part, wout_part, right_part = pl.pallas_call(
        main_kernel,
        out_shape=(
            jax.ShapeDtypeStruct((S, TI * C), BF16),
            jax.ShapeDtypeStruct((C * C, K), BF16),
            jax.ShapeDtypeStruct((4, 16, C * TJ), BF16),
        ),
        in_specs=[VMEM] * 7,
        out_specs=(VMEM,) * 3,
        scratch_shapes=[pltpu.VMEM((TI * C, C * TJ), BF16), pltpu.VMEM((C * C, K), F32)],
        compiler_params=pltpu.CompilerParams(vmem_limit_bytes=32 << 20),
        cost_estimate=pl.CostEstimate(flops=450_000_000, bytes_accessed=3_000_000, transcendentals=0),
    )(left_all, right_all, mask_j.astype(BF16), scaled, grad, right_keep, turn(right_give, "zb", 1))

    left_send = left_part.reshape(8, 16, 2, 8 * C).transpose(2, 0, 1, 3).reshape(1, 16, 32, K)
    send = jnp.concatenate(
        [
            jnp.broadcast_to(left_send, (2, 16, 32, K)).reshape(32, 32, K),
            wout_part.reshape(32, 32, K),
            jnp.broadcast_to(bias[None], (32, 8, K)),
        ],
        axis=1,
    )
    got = lax.all_to_all(send, NEAR, 0, 0, tiled=True)
    total = jnp.sum(got[:, 32:].astype(F32), axis=0)
    left_got = lax.dynamic_slice_in_dim(got, zb_at * 16, 16, 0)[:, :32]
    left_grad = jnp.sum(left_got.astype(F32), axis=0).reshape(16, 8, C)
    left_mask = lax.dynamic_slice(mask, (col_at * 16, row_at * 8), (16, 8))
    left_grad = (left_grad * left_mask.astype(F32)[:, :, None]).astype(BF16)
    bias_sum = total[32] + total[33]
    high = lax.reduce_precision(bias_sum, 8, 7)
    bias_rows = jnp.concatenate([high[None], (bias_sum - high)[None], jnp.zeros((6, K), F32)])
    rows = jnp.concatenate([total[:32], bias_rows]).astype(BF16)
    send = jnp.concatenate(
        [right_part.reshape(16, 32, K), jnp.broadcast_to(rows[None], (16, 40, K))], axis=1
    )
    got = lax.all_to_all(send, FAR, 0, 0, tiled=True).astype(F32)
    total = jnp.sum(got, axis=0)
    bias_sum = total[64] + total[65]
    right_sum = total[:32].reshape(1, 2, 1, 16, K).astype(BF16)
    rows = total[32:64].reshape(1, 1, 1, 32, K).astype(BF16)
    send = jnp.concatenate(
        [jnp.broadcast_to(rows, (2, 2, 8, 32, K)), jnp.broadcast_to(right_sum, (2, 2, 8, 16, K))], axis=3
    )
    got = lax.all_to_all(send.reshape(32, 48, K), NEAR, 0, 0, tiled=True)
    wout = got[:, :32].reshape(C * C, K).astype(F32)
    right_grad = lax.dynamic_slice(got.reshape(2, 2, 8, 48, K), (zb_at, 0, col_at, 32, 0), (1, 2, 1, 16, K))
    right_grad = right_grad.reshape(2, 2, C, TJ)
    right_mask = lax.dynamic_slice(mask, (row_at * 2, col_at * 64), (2, 64)).astype(BF16)
    right_grad = right_grad.transpose(1, 0, 3, 2).reshape(2, 64, C) * right_mask[:, :, None]
    return left_grad, right_grad, wout, bias_sum


def solution(mesh):
    parts = Mesh(mesh.devices.reshape(SHAPE), NAMES)
    left_spec, right_spec = P(COL, ROW, None), P(ROW, COL, None)
    return jax.shard_map(
        per_device,
        mesh=parts,
        in_specs=(left_spec, right_spec, P(), P(ROW, COL, None), P()),
        out_specs=(left_spec, right_spec, P(), P()),
        check_vma=False,
    )
```

time: 117 us -> 105 us (0.90)
  waiting for transfers between devices: 60.3 us -> 27.5 us
  blocking collectives: 0 us -> 20.3 us
  starting transfers between devices: 39.9 us -> 38.7 us
    all_to_all x5 -> x3, waiting for transfers between devices: 45.4 us -> 18.8 us  [the longest x1 10.8 us: per_device(): got = lax.all_to_all(send, NEAR, 0, 0, tiled=True)]
    all_to_all x0 -> x1, blocking collectives: none -> 20.3 us  [per_device(): got = lax.all_to_all(send, FAR, 0, 0, tiled=True).astype(F32)]
    all_to_all x5 -> x3, starting transfers between devices: 29 us -> 21.2 us  [the longest x1 10.4 us: per_device(): left_all = lax.all_to_all(send, ('core',) + COL, 0, 0, tiled=True)]
    all_to_all x1, waiting for transfers between devices: 14.9 us -> 8.65 us  [per_device(): right_all = lax.all_to_all(send, ROW, 0, 0, tiled=True).reshape(S, C * TJ)]
    ppermute x0 -> x2, starting transfers between devices: none -> 5.39 us  [turn(): return lax.ppermute(x, axis, [(i, (i + by) % n) for i in range(n)])]
    dynamic_slice x2 -> x3, local copies, waits for them, and re-layouts: 0.17 us -> 1.81 us  [the longest x1 0.92 us: per_device(): mask_i = lax.dynamic_slice_in_dim(mask, zy_at * TI, TI, 1)]
    all_to_all x1, starting transfers between devices: 10.9 us -> 12.1 us  [per_device(): right_all = lax.all_to_all(send, ROW, 0, 0, tiled=True).reshape(S, C * TJ)]
    convert_element_type x6 -> x4, other arithmetic: 2.3 us -> 2.55 us  [the longest x1 0.93 us: per_device(): mask_j.astype(BF16)]
  transfers between devices with their start and end apart: 6 -> 6, of which waited for: 5 -> 4; matrix products, arithmetic and copies ran while one was open for 5% -> 8% of each run, Pallas kernels for 1% -> 2%
where the time goes in v2:
time: 105 us
  starting transfers between devices  38.7 us (37%)
  waiting for transfers between devices  27.5 us (26%)
  blocking collectives  20.3 us (19%)
  other arithmetic  7.11 us (7%)
  local copies, waits for them, and re-layouts  6.24 us (6%)
  Pallas kernels  3.88 us (4%)
    all_to_all x1, blocking collectives, per_device(): got = lax.all_to_all(send, FAR, 0, 0, tiled=True).astype(F32)  20.3 us
    all_to_all x1, starting transfers between devices, per_device(): right_all = lax.all_to_all(send, ROW, 0, 0, tiled=True).reshape(S, C * TJ)  12.1 us
    all_to_all x1, waiting for transfers between devices, per_device(): got = lax.all_to_all(send, NEAR, 0, 0, tiled=True)  10.8 us
    all_to_all x1, starting transfers between devices, per_device(): left_all = lax.all_to_all(send, ('core',) + COL, 0, 0, tiled=True)  10.4 us
    all_to_all x1, waiting for transfers between devices, per_device(): right_all = lax.all_to_all(send, ROW, 0, 0, tiled=True).reshape(S, C * TJ)  8.65 us
    all_to_all x1, waiting for transfers between devices, per_device(): got = lax.all_to_all(send.reshape(32, 48, K), NEAR, 0, 0, tiled=True)  6.5 us
    all_to_all x1, starting transfers between devices, per_device(): got = lax.all_to_all(send.reshape(32, 48, K), NEAR, 0, 0, tiled=True)  6.3 us
    ppermute x2, starting transfers between devices, turn(): return lax.ppermute(x, axis, [(i, (i + by) % n) for i in range(n)])  5.39 us
  transfers between devices with their start and end apart: 6, of which 4 were waited for; matrix products, arithmetic and copies ran while one was open for 8% of the time, Pallas kernels for 2%

profile of v2, /device:TPU:1, one launch (start us, length us, event | category | flops | bytes accessed | tf_op | source)
XLA Modules:
  0.0 104.6 jit_solution(13647782762964299998)
XLA Ops:
  0.6 0.9 broadcast_in_dim.22
  2.2 10.4 %all-to-all-start = ((bf16[16,16,256]{2,1,0:T(8,128)(2,1)}), bf16[16,16,256]{2,1,0:T(8,128)(2,1)S(1)}, u32[]{:S(2)}, u32[]{:S(2)}) async-start(bf16[16,16,256]{2,1,0:T(8,128)(2,1)} %broadcast_in_dim.23), calls=%async_computation | async-start | bytes 262144 | tf_op jit(solution)/shard_map/all_to_all | solution.py:104
  12.5 0.9 constant_dynamic-slice_fusion.2
  13.4 2.1 %collective-permute-start = (bf16[8,32,128]{2,1,0:T(8,128)(2,1)S(1)}, bf16[8,32,128]{2,1,0:T(8,128)(2,1)S(1)}, u32[]{:S(2)}, u32[]{:S(2)}) collective-permute-start(bf16[8,32,128]{2,1,0:T(8,128)(2,1)S(1)} %get-tuple-element.24), channel_id=1, source_target_pairs={{0,8},{8,0},{1,9},{9,1},{2,10},{10,2},{3,11},{11,3},{4,12},{12,4},... | collective-permute-start | bytes 196616 | tf_op jit(solution)/shard_map/ppermute | solution.py:94
  15.5 0.8 reshape.103
  16.4 0.9 dynamic-slice_convert_fusion
  17.4 1.5 %all-to-all-done.l_in = bf16[16,16,256]{2,1,0:T(8,128)(2,1)S(1)} async-done(((bf16[16,16,256]{2,1,0:T(8,128)(2,1)}), bf16[16,16,256]{2,1,0:T(8,128)(2,1)S(1)}, u32[]{:S(2)}, u32[]{:S(2)}) %all-to-all-start) | async-done | bytes 131104 | tf_op jit(solution)/shard_map/all_to_all | solution.py:104
  18.9 0.8 broadcast_in_dim.25
  19.7 12.1 %all-to-all-start.1 = ((bf16[64,2,1024]{2,1,0:T(2,128)(2,1)}), bf16[64,2,1024]{2,1,0:T(2,128)(2,1)S(1)}, u32[]{:S(2)}, u32[]{:S(2)}) async-start(bf16[64,2,1024]{2,1,0:T(2,128)(2,1)} %bitcast.9), calls=%async_computation.1 | async-start | bytes 524288 | tf_op jit(solution)/shard_map/all_to_all | solution.py:108
  31.8 0.9 constant_dynamic-slice_fusion.1
  33.3 2.1 %shard_map.84 = (bf16[512,128]{1,0:T(8,128)(2,1)S(1)}, bf16[8,128]{1,0:T(8,128)(2,1)S(1)}, bf16[512,1024]{1,0:T(8,128)(2,1)S(1)}, bf16[128,512]{1,0:T(8,128)(2,1...) custom-call(s32[2]{0:T(128)S(1)} %pad_add_fusion.at_ref, ...), custom_call_target="tpu_custom_call" | custom-call | flops 300000000 | bytes 3000000 | tf_op jit(solution)/shard_map/pallas_call | solution.py:117
  35.3 3.3 %collective-permute-start.1 = (bf16[4,16,1024]{2,1,0:T(8,128)(2,1)S(1)}, bf16[4,16,1024]{2,1,0:T(8,128)(2,1)S(1)}, u32[]{:S(2)}, u32[]{:S(2)}) collective-permute-start(bf16[4,16,1024]{2,1,0:T(8,128)(2,1)S(1)} %get-tuple-element.17), channel_id=1, source_target_pairs={{0,64},{64,0},{1,65},{65,1},{2,66},{66,2},{3,67},{67,3},{4,68},{68... | collective-permute-start | bytes 393224 | tf_op jit(solution)/shard_map/ppermute | solution.py:94
  38.6 8.6 %all-to-all-done.1 = bf16[64,2,1024]{2,1,0:T(2,128)(2,1)S(1)} async-done(((bf16[64,2,1024]{2,1,0:T(2,128)(2,1)}), bf16[64,2,1024]{2,1,0:T(2,128)(2,1)S(1)}, u32[]{:S(2)}, u32[]{:S(2)}) %all-to-all-start.1) | async-done | bytes 262176 | tf_op jit(solution)/shard_map/all_to_all | solution.py:108
  47.4 1.8 %shard_map.85 = (bf16[128,512]{1,0:T(8,128)(2,1)S(1)}, bf16[1024,128]{1,0:T(8,128)(2,1)S(1)}, bf16[4,16,1024]{2,1,0:T(8,128)(2,1)S(1)}) custom-call(bf16[128,512]{1,0:T(8,128)(2,1)S(1)} %get-tuple-element.13.l_ref, bf16[128,1024]{1,0:T(8,128)(2,1)S(1)} %reshape.105.r_ref, bf16[128,32]{1,0:T(8,128)(2,1)S(1)} %get-tuple-element.22.m_ref, ...), custom_call_target="tpu_custom_call" | custom-call | flops 450000000 | bytes 3000000 | tf_op jit(solution)/shard_map/pallas_call | solution.py:135
  49.4 0.9 pad_maximum_fusion
  50.3 4.5 %all-to-all-start.2 = ((bf16[32,72,128]{2,1,0:T(8,128)(2,1)}), bf16[32,72,128]{2,1,0:T(8,128)(2,1)S(1)}, u32[]{:S(2)}, u32[]{:S(2)}) async-start(bf16[32,72,128]{2,1,0:T(8,128)(2,1)} %pad_maximum_fusion), calls=%async_computation.2 | async-start | bytes 1179648 | tf_op jit(solution)/shard_map/all_to_all | solution.py:158
  55.0 10.8 %all-to-all-done.2 = bf16[32,72,128]{2,1,0:T(8,128)(2,1)S(1)} async-done(((bf16[32,72,128]{2,1,0:T(8,128)(2,1)}), bf16[32,72,128]{2,1,0:T(8,128)(2,1)S(1)}, u32[]{:S(2)}, u32[]{:S(2)}) %all-to-all-start.2) | async-done | bytes 589856 | tf_op jit(solution)/shard_map/all_to_all | solution.py:158
  66.0 20.3 %all_to_all.25 = bf16[16,72,128]{2,1,0:T(8,128)(2,1)S(1)} all-to-all(bf16[16,72,128]{2,1,0:T(8,128)(2,1)S(1)} %pad_maximum_fusion.2), channel_id=1, replica_groups=mesh['zq'=4,'zb'=2,'yh'=4,'core'=2,'yl'=2,'x'=4] {'zq','yh'}, dimensions={0} | all-to-all | bytes 589824 | tf_op jit(solution)/shard_map/all_to_all | solution.py:171
  86.4 0.8 pad_maximum_fusion.1
  87.2 6.3 %all-to-all-start.4 = ((bf16[32,48,128]{2,1,0:T(8,128)(2,1)}), bf16[32,48,128]{2,1,0:T(8,128)(2,1)S(1)}, u32[]{:S(2)}, u32[]{:S(2)}) async-start(bf16[32,48,128]{2,1,0:T(8,128)(2,1)} %bitcast.14), calls=%async_computation.4 | async-start | bytes 786432 | tf_op jit(solution)/shard_map/all_to_all | solution.py:179
  93.5 0.8 dynamic-slice_convert_fusion.2
  94.3 0.8 dynamic-slice_convert_fusion.1
  96.4 6.5 %all-to-all-done.4 = bf16[32,48,128]{2,1,0:T(8,128)(2,1)S(1)} async-done(((bf16[32,48,128]{2,1,0:T(8,128)(2,1)}), bf16[32,48,128]{2,1,0:T(8,128)(2,1)S(1)}, u32[]{:S(2)}, u32[]{:S(2)}) %all-to-all-start.4) | async-done | bytes 393248 | tf_op jit(solution)/shard_map/all_to_all | solution.py:179
  102.9 0.8 bitcast_convert_fusion
  (43 shorter events, 4.1 us)
Async XLA Ops:
  2.2 30.9 %copy-start = (bf16[1024,128]{1,0:T(8,128)(2,1)S(1)}, bf16[1024,128]{1,0:T(8,128)(2,1)}, u32[]{:S(2)}) copy-start(bf16[1024,128]{1,0:T(8,128)(2,1)} %param.7) | copy-start | bytes 786436
  2.2 16.7 %all-to-all-start = ((bf16[16,16,256]{2,1,0:T(8,128)(2,1)}), bf16[16,16,256]{2,1,0:T(8,128)(2,1)S(1)}, u32[]{:S(2)}, u32[]{:S(2)}) async-start(bf16[16,16,256]{2,1,0:T(8,128)(2,1)} %broadcast_in_dim.23), calls=%async_computation | async-start | bytes 262144 | tf_op jit(solution)/shard_map/all_to_all | solution.py:104
  13.4 19.9 %collective-permute-start = (bf16[8,32,128]{2,1,0:T(8,128)(2,1)S(1)}, bf16[8,32,128]{2,1,0:T(8,128)(2,1)S(1)}, u32[]{:S(2)}, u32[]{:S(2)}) collective-permute-start(bf16[8,32,128]{2,1,0:T(8,128)(2,1)S(1)} %get-tuple-element.24), channel_id=1, source_target_pairs={{0,8},{8,0},{1,9},{9,1},{2,10},{10,2},{3,11},{11,3},{4,12},{12,4},... | collective-permute-start | bytes 196616 | tf_op jit(solution)/shard_map/ppermute | solution.py:94
  19.7 27.6 %all-to-all-start.1 = ((bf16[64,2,1024]{2,1,0:T(2,128)(2,1)}), bf16[64,2,1024]{2,1,0:T(2,128)(2,1)S(1)}, u32[]{:S(2)}, u32[]{:S(2)}) async-start(bf16[64,2,1024]{2,1,0:T(2,128)(2,1)} %bitcast.9), calls=%async_computation.1 | async-start | bytes 524288 | tf_op jit(solution)/shard_map/all_to_all | solution.py:108
  35.3 12.1 %collective-permute-start.1 = (bf16[4,16,1024]{2,1,0:T(8,128)(2,1)S(1)}, bf16[4,16,1024]{2,1,0:T(8,128)(2,1)S(1)}, u32[]{:S(2)}, u32[]{:S(2)}) collective-permute-start(bf16[4,16,1024]{2,1,0:T(8,128)(2,1)S(1)} %get-tuple-element.17), channel_id=1, source_target_pairs={{0,64},{64,0},{1,65},{65,1},{2,66},{66,2},{3,67},{67,3},{4,68},{68... | collective-permute-start | bytes 393224 | tf_op jit(solution)/shard_map/ppermute | solution.py:94
  50.3 15.5 %all-to-all-start.2 = ((bf16[32,72,128]{2,1,0:T(8,128)(2,1)}), bf16[32,72,128]{2,1,0:T(8,128)(2,1)S(1)}, u32[]{:S(2)}, u32[]{:S(2)}) async-start(bf16[32,72,128]{2,1,0:T(8,128)(2,1)} %pad_maximum_fusion), calls=%async_computation.2 | async-start | bytes 1179648 | tf_op jit(solution)/shard_map/all_to_all | solution.py:158
  87.2 15.7 %all-to-all-start.4 = ((bf16[32,48,128]{2,1,0:T(8,128)(2,1)}), bf16[32,48,128]{2,1,0:T(8,128)(2,1)S(1)}, u32[]{:S(2)}, u32[]{:S(2)}) async-start(bf16[32,48,128]{2,1,0:T(8,128)(2,1)} %bitcast.14), calls=%async_computation.4 | async-start | bytes 786432 | tf_op jit(solution)/shard_map/all_to_all | solution.py:179

commit v3 on v2

--- a/solution.py
+++ b/solution.py
@@ -26,6 +26,13 @@
     return lax.dot_general(a, b, (((ca,), (cb,)), ((), ())), preferred_element_type=F32)
 
 
+def copies_kernel(l_ref, send_ref):
+    left = l_ref[...].astype(F32)
+    left = jnp.concatenate([left[:, i, :] for i in range(8)], axis=1).astype(BF16)
+    for to in range(16):
+        send_ref[to] = left
+
+
 def scale_kernel(
     at_ref, keep_ref, take_ref, m_ref, mi_ref, mj_ref, w_ref, l_in,
     s_ref, bias_ref, g_ref, l_ref, rkeep_ref, rgive_ref, right_ref,
@@ -39,7 +46,7 @@
     scaled = pair.reshape(TI * TJ, K).astype(F32) / jnp.maximum(counts, 1.0)
     total = jnp.sum(scaled, axis=0, keepdims=True)
     high = total.astype(BF16).astype(F32)
-    row = lax.broadcasted_iota(jnp.int32, (8, K), 0)
+    row = lax.broadcasted_iota(jnp.int32, (16, K), 0)
     bias_ref[...] = jnp.where(row == 0, high, jnp.where(row == 1, total - high, 0.0)).astype(BF16)
     scaled = scaled.astype(BF16)
     s_ref[...] = scaled
@@ -67,9 +74,8 @@
 
 
 def main_kernel(
-    l_ref, r_ref, m_ref, s_ref, g_ref, rkeep_ref, rtake_ref, left_ref, wout_ref, rsum_ref, o_ref, w_ref
+    l_ref, r_ref, m_ref, s_ref, g_ref, bias_ref, send_ref, o_ref, w_ref, left_ref
 ):
-    rsum_ref[...] = (rkeep_ref[...].astype(F32) + rtake_ref[...].astype(F32)).astype(BF16)
     right = r_ref[...] * jnp.concatenate([m_ref[...]] * C, axis=1)
     o_ref[...] = dot(l_ref[...], right, 0, 0).astype(BF16)
     pairs = s_ref[...]
@@ -85,8 +91,47 @@
         outer = jnp.concatenate(rows, axis=0)
         w_ref[g * 4 * C : (g + 1) * 4 * C, :] = dot(outer, pairs, 1, 0)
     for c in range(C):
-        wout_ref[c * C : (c + 1) * C, :] = w_ref[pl.ds(c, C, stride=C), :].astype(BF16)
+        send_ref[c, 32:64, :] = w_ref[pl.ds(c, C, stride=C), :].astype(BF16)
+        send_ref[c, 64:80, :] = bias_ref[...]
     left_ref[...] = dot(right, g_ref[...], 1, 1).astype(BF16)
+    for zb in range(2):
+        for core in range(2):
+            for col in range(8):
+                for h in range(2):
+                    at = core * 8 * C + h * K
+                    send_ref[zb * 16 + core * 8 + col, h * 16 : (h + 1) * 16, :] = left_ref[
+                        col * 16 : (col + 1) * 16, at : at + K
+                    ]
+
+
+def join_kernel(got_ref, l_ref, ml_ref, send_ref, left_ref, bias_ref):
+    total = got_ref[0].astype(F32)
+    for source in range(1, 16):
+        total = total + got_ref[source].astype(F32)
+    bias_ref[...] = total[64:65] + total[65:66]
+    rows = total[:64].astype(BF16)
+    for zb in range(2):
+        for core in range(2):
+            for col in range(8):
+                to = zb * 16 + core * 8 + col
+                send_ref[to, :32, :] = rows[32:64]
+                send_ref[to, 32:48, :] = rows[core * 16 : (core + 1) * 16]
+    lane = lax.broadcasted_iota(jnp.int32, (8, 8 * C), 1) // C
+    spread = (lane == lax.broadcasted_iota(jnp.int32, (8, 8 * C), 0)).astype(BF16)
+    left = jnp.concatenate([l_ref[:16, :], l_ref[16:, :]], axis=1)
+    left_ref[...] = (left * dot(ml_ref[...], spread, 1, 0)).astype(BF16)
+
+
+def tail_kernel(at_ref, got_ref, m_ref, wout_ref, right_ref, turned_ref):
+    for c in range(C):
+        wout_ref[c * C : (c + 1) * C, :] = got_ref[c, :32, :].astype(F32)
+    near, far = [got_ref[at_ref[0] + core * 8, 32:48, :].astype(F32) for core in range(2)]
+    for q in range(2):
+        for e in range(4):
+            rows, lanes = slice(q * 8, (q + 1) * 8), slice(e * TJ, (e + 1) * TJ)
+            piece = jnp.concatenate([near[rows, lanes], far[rows, lanes]], axis=1)
+            turned_ref[q, pl.ds(e, 8, stride=4), :] = piece
+    right_ref[...] = (turned_ref[...] * m_ref[...][:, None, :]).astype(BF16)
 
 
 def turn(x, axis, by):
@@ -100,11 +145,18 @@
     col_at = lax.axis_index(COL)
     core_at = lax.axis_index("core")
     zb_at = lax.axis_index("zb")
-    send = jnp.broadcast_to(left.reshape(1, 16, 8 * C), (16, 16, 8 * C))
+    send = pl.pallas_call(
+        copies_kernel,
+        out_shape=jax.ShapeDtypeStruct((16, 16, 8 * C), BF16),
+        in_specs=[VMEM],
+        out_specs=VMEM,
+        compiler_params=pltpu.CompilerParams(vmem_limit_bytes=16 << 20),
+    )(left)
     left_all = lax.all_to_all(send, ("core",) + COL, 0, 0, tiled=True)
     send = right.transpose(0, 2, 1).reshape(2, C, 2, TJ)
     send = send.transpose(2, 0, 1, 3).reshape(1, 2, 2, C * TJ)
     send = jnp.broadcast_to(send, (32, 2, 2, C * TJ)).reshape(64, 2, C * TJ)
+    send, pair = lax.optimization_barrier((send, pair))
     right_all = lax.all_to_all(send, ROW, 0, 0, tiled=True).reshape(S, C * TJ)
     keep = lax.dynamic_slice_in_dim(pair, core_at * TJ, TJ, 1)
     give = lax.dynamic_slice_in_dim(pair, (1 - core_at) * TJ, TJ, 1)
@@ -118,7 +170,7 @@
         scale_kernel,
         out_shape=(
             jax.ShapeDtypeStruct((TI * TJ, K), BF16),
-            jax.ShapeDtypeStruct((8, K), BF16),
+            jax.ShapeDtypeStruct((16, K), BF16),
             jax.ShapeDtypeStruct((TI * C, C * TJ), BF16),
             jax.ShapeDtypeStruct((S, TI * C), BF16),
             jax.ShapeDtypeStruct((4, 16, C * TJ), BF16),
@@ -132,35 +184,28 @@
     )(
         at, keep, take, mask_i.astype(BF16), mask_i.T.astype(F32), mask_j.T.astype(F32), weight, left_all
     )
-    left_part, wout_part, right_part = pl.pallas_call(
+    right_take = turn(right_give, "zb", 1)
+    right_take, right_all = lax.optimization_barrier((right_take, right_all))
+    right_part = (right_keep.astype(F32) + right_take.astype(F32)).astype(BF16)
+    send = pl.pallas_call(
         main_kernel,
-        out_shape=(
-            jax.ShapeDtypeStruct((S, TI * C), BF16),
-            jax.ShapeDtypeStruct((C * C, K), BF16),
-            jax.ShapeDtypeStruct((4, 16, C * TJ), BF16),
-        ),
-        in_specs=[VMEM] * 7,
-        out_specs=(VMEM,) * 3,
-        scratch_shapes=[pltpu.VMEM((TI * C, C * TJ), BF16), pltpu.VMEM((C * C, K), F32)],
+        out_shape=jax.ShapeDtypeStruct((32, 80, K), BF16),
+        in_specs=[VMEM] * 6,
+        out_specs=VMEM,
+        scratch_shapes=[
+            pltpu.VMEM((TI * C, C * TJ), BF16),
+            pltpu.VMEM((C * C, K), F32),
+            pltpu.VMEM((S, TI * C), BF16),
+        ],
         compiler_params=pltpu.CompilerParams(vmem_limit_bytes=32 << 20),
         cost_estimate=pl.CostEstimate(flops=450_000_000, bytes_accessed=3_000_000, transcendentals=0),
-    )(left_all, right_all, mask_j.astype(BF16), scaled, grad, right_keep, turn(right_give, "zb", 1))
-
-    left_send = left_part.reshape(8, 16, 2, 8 * C).transpose(2, 0, 1, 3).reshape(1, 16, 32, K)
-    send = jnp.concatenate(
-        [
-            jnp.broadcast_to(left_send, (2, 16, 32, K)).reshape(32, 32, K),
-            wout_part.reshape(32, 32, K),
-            jnp.broadcast_to(bias[None], (32, 8, K)),
-        ],
-        axis=1,
-    )
+    )(left_all, right_all, mask_j.astype(BF16), scaled, grad, bias)
+
     got = lax.all_to_all(send, NEAR, 0, 0, tiled=True)
-    total = jnp.sum(got[:, 32:].astype(F32), axis=0)
+    total = jnp.sum(got[:, 32:72].astype(F32), axis=0)
     left_got = lax.dynamic_slice_in_dim(got, zb_at * 16, 16, 0)[:, :32]
-    left_grad = jnp.sum(left_got.astype(F32), axis=0).reshape(16, 8, C)
-    left_mask = lax.dynamic_slice(mask, (col_at * 16, row_at * 8), (16, 8))
-    left_grad = (left_grad * left_mask.astype(F32)[:, :, None]).astype(BF16)
+    left_sum = jnp.sum(left_got.astype(F32), axis=0)
+    left_mask = lax.dynamic_slice(mask, (col_at * 16, row_at * 8), (16, 8)).astype(BF16)
     bias_sum = total[32] + total[33]
     high = lax.reduce_precision(bias_sum, 8, 7)
     bias_rows = jnp.concatenate([high[None], (bias_sum - high)[None], jnp.zeros((6, K), F32)])
@@ -168,20 +213,35 @@
     send = jnp.concatenate(
         [right_part.reshape(16, 32, K), jnp.broadcast_to(rows[None], (16, 40, K))], axis=1
     )
-    got = lax.all_to_all(send, FAR, 0, 0, tiled=True).astype(F32)
-    total = jnp.sum(got, axis=0)
-    bias_sum = total[64] + total[65]
-    right_sum = total[:32].reshape(1, 2, 1, 16, K).astype(BF16)
-    rows = total[32:64].reshape(1, 1, 1, 32, K).astype(BF16)
-    send = jnp.concatenate(
-        [jnp.broadcast_to(rows, (2, 2, 8, 32, K)), jnp.broadcast_to(right_sum, (2, 2, 8, 16, K))], axis=3
-    )
-    got = lax.all_to_all(send.reshape(32, 48, K), NEAR, 0, 0, tiled=True)
-    wout = got[:, :32].reshape(C * C, K).astype(F32)
-    right_grad = lax.dynamic_slice(got.reshape(2, 2, 8, 48, K), (zb_at, 0, col_at, 32, 0), (1, 2, 1, 16, K))
-    right_grad = right_grad.reshape(2, 2, C, TJ)
-    right_mask = lax.dynamic_slice(mask, (row_at * 2, col_at * 64), (2, 64)).astype(BF16)
-    right_grad = right_grad.transpose(1, 0, 3, 2).reshape(2, 64, C) * right_mask[:, :, None]
+    got = lax.all_to_all(send, FAR, 0, 0, tiled=True)
+    send, left_grad, bias_sum = pl.pallas_call(
+        join_kernel,
+        out_shape=(
+            jax.ShapeDtypeStruct((32, 48, K), BF16),
+            jax.ShapeDtypeStruct((16, 8 * C), BF16),
+            jax.ShapeDtypeStruct((1, K), F32),
+        ),
+        in_specs=[VMEM] * 3,
+        out_specs=(VMEM,) * 3,
+        compiler_params=pltpu.CompilerParams(vmem_limit_bytes=16 << 20),
+    )(got, left_sum, left_mask)
+    left_grad = left_grad.reshape(16, 8, C)
+    bias_sum = bias_sum.reshape(K)
+    got = lax.all_to_all(send, NEAR, 0, 0, tiled=True)
+    right_mask = lax.dynamic_slice(mask, (row_at * 2, col_at * 64), (2, 64)).astype(F32)
+    at = (zb_at * 16 + col_at).reshape(1).astype(jnp.int32)
+    wout, right_grad = pl.pallas_call(
+        tail_kernel,
+        out_shape=(
+            jax.ShapeDtypeStruct((C * C, K), F32),
+            jax.ShapeDtypeStruct((2, C, 64), BF16),
+        ),
+        in_specs=[SMEM] + [VMEM] * 2,
+        out_specs=(VMEM,) * 2,
+        scratch_shapes=[pltpu.VMEM((2, C, 64), F32)],
+        compiler_params=pltpu.CompilerParams(vmem_limit_bytes=16 << 20),
+    )(at, got, right_mask)
+    right_grad = right_grad.transpose(0, 2, 1)
     return left_grad, right_grad, wout, bias_sum
 
 

time: 105 us -> 104 us (level)
  blocking collectives: 20.3 us -> 0 us
  waiting for transfers between devices: 27.5 us -> 44.5 us
  starting transfers between devices: 38.7 us -> 45 us
  other arithmetic: 7.11 us -> 1.28 us
  Pallas kernels: 3.88 us -> 7.17 us
  local copies, waits for them, and re-layouts: 6.24 us -> 4.56 us
    all_to_all x1 -> x0, blocking collectives: 20.3 us -> none  [per_device(): got = lax.all_to_all(send, FAR, 0, 0, tiled=True).astype(F32)]
    all_to_all x1 -> x2, waiting for transfers between devices: 10.8 us -> 19.9 us  [per_device(): got = lax.all_to_all(send, NEAR, 0, 0, tiled=True)]
    all_to_all x1, waiting for transfers between devices: 6.5 us -> 13.3 us  [per_device(): got = lax.all_to_all(send, FAR, 0, 0, tiled=True)]
    all_to_all x1 -> x2, starting transfers between devices: 4.55 us -> 10.5 us  [per_device(): got = lax.all_to_all(send, NEAR, 0, 0, tiled=True)]
    pallas_call x1 -> x4, Pallas kernels: 1.8 us -> 5.09 us  [the longest x1 2.67 us: per_device(): pl.pallas_call(main_kernel, out_shape=jax.ShapeDtypeStruct((32, 80, K), B...]
    convert_element_type x4 -> x3, other arithmetic: 3.09 us -> 0.2 us  [the longest x1 0.08 us: per_device(): lax.dynamic_slice(mask, (col_at * 16, row_at * 8), (16, 8)).astype(BF16)]
    unnamed x3 -> x11, local copies, waits for them, and re-layouts: 0.07 us -> 2.15 us
    broadcast_in_dim x7 -> x0, local copies, waits for them, and re-layouts: 1.67 us -> none  [the longest x2 1.52 us: per_device(): send = jnp.broadcast_to(left.reshape(1, 16, 8 * C), (16, 16, 8 * C))]
  transfers between devices with their start and end apart: 6 -> 7, of which waited for: 4 -> 5; matrix products, arithmetic and copies ran while one was open for 8% -> 3% of each run, Pallas kernels for 2% -> 2%
where the time goes in v3:
time: 104 us; the launch traced here: 103 us
  starting transfers between devices  45 us (43%)
  waiting for transfers between devices  44.5 us (43%)
  Pallas kernels  7.17 us (7%)
  local copies, waits for them, and re-layouts  4.56 us (4%)
  other arithmetic  1.28 us (1%)
    all_to_all x2, waiting for transfers between devices, per_device(): got = lax.all_to_all(send, NEAR, 0, 0, tiled=True)  19.9 us
    all_to_all x1, waiting for transfers between devices, per_device(): got = lax.all_to_all(send, FAR, 0, 0, tiled=True)  13.3 us
    all_to_all x1, starting transfers between devices, per_device(): right_all = lax.all_to_all(send, ROW, 0, 0, tiled=True).reshape(S, C * TJ)  12.1 us
    all_to_all x2, starting transfers between devices, per_device(): got = lax.all_to_all(send, NEAR, 0, 0, tiled=True)  10.5 us
    all_to_all x1, starting transfers between devices, per_device(): left_all = lax.all_to_all(send, ('core',) + COL, 0, 0, tiled=True)  10.2 us
    all_to_all x1, waiting for transfers between devices, per_device(): right_all = lax.all_to_all(send, ROW, 0, 0, tiled=True).reshape(S, C * TJ)  8.92 us
    all_to_all x1, starting transfers between devices, per_device(): got = lax.all_to_all(send, FAR, 0, 0, tiled=True)  6.76 us
    ppermute x2, starting transfers between devices, turn(): return lax.ppermute(x, axis, [(i, (i + by) % n) for i in range(n)])  5.38 us
  transfers between devices with their start and end apart: 7, of which 5 were waited for; matrix products, arithmetic and copies ran while one was open for 3% of the time, Pallas kernels for 2%

profile of v3, /device:TPU:1, one launch (start us, length us, event | category | flops | bytes accessed | tf_op | source)
XLA Modules:
  0.0 103.3 jit_solution(3663161436131083448)
XLA Ops:
  0.6 0.7 copy-done
  1.4 0.8 shard_map.84
  2.2 10.2 %all-to-all-start = ((bf16[16,16,256]{2,1,0:T(8,128)(2,1)}), bf16[16,16,256]{2,1,0:T(8,128)(2,1)S(1)}, u32[]{:S(2)}, u32[]{:S(2)}) async-start(bf16[16,16,256]{2,1,0:T(8,128)(2,1)} %shard_map.84), calls=%async_computation | async-start | bytes 262144 | tf_op jit(solution)/shard_map/all_to_all | solution.py:155
  12.4 0.7 copy-done.4
  13.3 0.8 broadcast_in_dim.9
  14.2 2.1 %collective-permute-start = (bf16[8,32,128]{2,1,0:T(8,128)(2,1)S(1)}, bf16[8,32,128]{2,1,0:T(8,128)(2,1)S(1)}, u32[]{:S(2)}, u32[]{:S(2)}) collective-permute-start(bf16[8,32,128]{2,1,0:T(8,128)(2,1)S(1)} %get-tuple-element.36), channel_id=1, source_target_pairs={{0,8},{8,0},{1,9},{9,1},{2,10},{10,2},{3,11},{11,3},{4,12},{12,4},... | collective-permute-start | bytes 196616 | tf_op jit(solution)/shard_map/ppermute | solution.py:139
  16.4 2.3 %all-to-all-done.l_in = bf16[16,16,256]{2,1,0:T(8,128)(2,1)S(1)} async-done(((bf16[16,16,256]{2,1,0:T(8,128)(2,1)}), bf16[16,16,256]{2,1,0:T(8,128)(2,1)S(1)}, u32[]{:S(2)}, u32[]{:S(2)}) %all-to-all-start) | async-done | bytes 131104 | tf_op jit(solution)/shard_map/all_to_all | solution.py:155
  18.7 12.1 %all-to-all-start.1 = ((bf16[64,2,1024]{2,1,0:T(2,128)(2,1)}), bf16[64,2,1024]{2,1,0:T(2,128)(2,1)S(1)}, u32[]{:S(2)}, u32[]{:S(2)}) async-start(bf16[64,2,1024]{2,1,0:T(2,128)(2,1)} %bitcast.4), calls=%async_computation.1 | async-start | bytes 524288 | tf_op jit(solution)/shard_map/all_to_all | solution.py:160
  31.1 0.1 copy.16.m_ref
  31.3 0.6 copy-done.1
  32.0 2.1 %shard_map.85 = (bf16[512,128]{1,0:T(8,128)(2,1)S(1)}, bf16[16,128]{1,0:T(8,128)(2,1)S(1)}, bf16[512,1024]{1,0:T(8,128)(2,1)S(1)}, bf16[128,512]{1,0:T(8,128)(2,...) custom-call(s32[2]{0:T(128)S(1)} %pad_add_fusion.at_ref, ...), custom_call_target="tpu_custom_call" | custom-call | flops 300000000 | bytes 3000000 | tf_op jit(solution)/shard_map/pallas_call | solution.py:169
  34.1 3.3 %collective-permute-start.1 = (bf16[4,16,1024]{2,1,0:T(8,128)(2,1)S(1)}, bf16[4,16,1024]{2,1,0:T(8,128)(2,1)S(1)}, u32[]{:S(2)}, u32[]{:S(2)}) collective-permute-start(bf16[4,16,1024]{2,1,0:T(8,128)(2,1)S(1)} %get-tuple-element.21), channel_id=1, source_target_pairs={{0,64},{64,0},{1,65},{65,1},{2,66},{66,2},{3,67},{67,3},{4,68},{68... | collective-permute-start | bytes 393224 | tf_op jit(solution)/shard_map/ppermute | solution.py:139
  37.4 8.9 %all-to-all-done.1 = bf16[64,2,1024]{2,1,0:T(2,128)(2,1)S(1)} async-done(((bf16[64,2,1024]{2,1,0:T(2,128)(2,1)}), bf16[64,2,1024]{2,1,0:T(2,128)(2,1)S(1)}, u32[]{:S(2)}, u32[]{:S(2)}) %all-to-all-start.1) | async-done | bytes 262176 | tf_op jit(solution)/shard_map/all_to_all | solution.py:160
  46.5 2.7 %shard_map.86 = bf16[32,80,128]{2,1,0:T(8,128)(2,1)} custom-call(bf16[128,512]{1,0:T(8,128)(2,1)S(1)} %get-tuple-element.24.l_ref, bf16[128,1024]{1,0:T(8,128)(2,1)S(1)} %reshape.67.r_ref, bf16[128,32]{1,0:T(8,128)(2,1)S(1)} %get-tuple-element.34.m_ref, bf16[512,128]{1,0:T(8,128)(2,1)S(1)} %get-tuple-element.26.s_ref, ...), custom_call_target="tpu_custom_call" | custom-call | flops 450000000 | bytes 3000000 | tf_op jit(solution)/shard_map/pallas_call | solution.py:190
  49.1 3.9 %all-to-all-start.2 = ((bf16[32,80,128]{2,1,0:T(8,128)(2,1)}), bf16[32,80,128]{2,1,0:T(8,128)(2,1)S(1)}, u32[]{:S(2)}, u32[]{:S(2)}) async-start(bf16[32,80,128]{2,1,0:T(8,128)(2,1)} %shard_map.86), calls=%async_computation.2 | async-start | bytes 1310720 | tf_op jit(solution)/shard_map/all_to_all | solution.py:204
  53.2 11.4 %all-to-all-done.2 = bf16[32,80,128]{2,1,0:T(8,128)(2,1)S(1)} async-done(((bf16[32,80,128]{2,1,0:T(8,128)(2,1)}), bf16[32,80,128]{2,1,0:T(8,128)(2,1)S(1)}, u32[]{:S(2)}, u32[]{:S(2)}) %all-to-all-start.2) | async-done | bytes 655392 | tf_op jit(solution)/shard_map/all_to_all | solution.py:204
  64.8 0.7 pad_maximum_fusion
  65.5 6.8 %all-to-all-start.3 = ((bf16[16,72,128]{2,1,0:T(8,128)(2,1)}), bf16[16,72,128]{2,1,0:T(8,128)(2,1)S(1)}, u32[]{:S(2)}, u32[]{:S(2)}) async-start(bf16[16,72,128]{2,1,0:T(8,128)(2,1)} %pad_maximum_fusion), calls=%async_computation.3 | async-start | bytes 589824 | tf_op jit(solution)/shard_map/all_to_all | solution.py:216
  72.4 13.3 %all-to-all-done.3.got_ref = bf16[16,72,128]{2,1,0:T(8,128)(2,1)S(1)} async-done(((bf16[16,72,128]{2,1,0:T(8,128)(2,1)}), bf16[16,72,128]{2,1,0:T(8,128)(2,1)S(1)}, u32[]{:S(2)}, u32[]{:S(2)}) %all-to-all-start.3) | async-done | bytes 294944 | tf_op jit(solution)/shard_map/all_to_all | solution.py:216
  85.7 0.8 shard_map.87
  86.5 6.6 %all-to-all-start.4 = ((bf16[32,48,128]{2,1,0:T(8,128)(2,1)}), bf16[32,48,128]{2,1,0:T(8,128)(2,1)S(1)}, u32[]{:S(2)}, u32[]{:S(2)}) async-start(bf16[32,48,128]{2,1,0:T(8,128)(2,1)} %get-tuple-element.30), calls=%async_computation.4 | async-start | bytes 786432 | tf_op jit(solution)/shard_map/all_to_all | solution.py:230
  93.2 0.7 reshape.69
  93.9 8.6 %all-to-all-done.4.got_ref = bf16[32,48,128]{2,1,0:T(8,128)(2,1)S(1)} async-done(((bf16[32,48,128]{2,1,0:T(8,128)(2,1)}), bf16[32,48,128]{2,1,0:T(8,128)(2,1)S(1)}, u32[]{:S(2)}, u32[]{:S(2)}) %all-to-all-start.4) | async-done | bytes 393248 | tf_op jit(solution)/shard_map/all_to_all | solution.py:230
  102.5 0.8 shard_map.88
  (33 shorter events, 1.4 us)
Async XLA Ops:
  0.6 0.8 copy-start
  2.2 16.6 %all-to-all-start = ((bf16[16,16,256]{2,1,0:T(8,128)(2,1)}), bf16[16,16,256]{2,1,0:T(8,128)(2,1)S(1)}, u32[]{:S(2)}, u32[]{:S(2)}) async-start(bf16[16,16,256]{2,1,0:T(8,128)(2,1)} %shard_map.84), calls=%async_computation | async-start | bytes 262144 | tf_op jit(solution)/shard_map/all_to_all | solution.py:155
  12.4 0.7 copy-start.4
  13.3 0.9 copy-start.2
  13.3 3.0 %copy-start.3 = (s32[128,512]{1,0:T(8,128)S(1)}, s32[128,512]{1,0:T(8,128)}, u32[]{:S(2)}) copy-start(s32[128,512]{1,0:T(8,128)} %param.9) | copy-start | bytes 786436
  14.2 17.8 %collective-permute-start = (bf16[8,32,128]{2,1,0:T(8,128)(2,1)S(1)}, bf16[8,32,128]{2,1,0:T(8,128)(2,1)S(1)}, u32[]{:S(2)}, u32[]{:S(2)}) collective-permute-start(bf16[8,32,128]{2,1,0:T(8,128)(2,1)S(1)} %get-tuple-element.36), channel_id=1, source_target_pairs={{0,8},{8,0},{1,9},{9,1},{2,10},{10,2},{3,11},{11,3},{4,12},{12,4},... | collective-permute-start | bytes 196616 | tf_op jit(solution)/shard_map/ppermute | solution.py:139
  18.7 27.6 %all-to-all-start.1 = ((bf16[64,2,1024]{2,1,0:T(2,128)(2,1)}), bf16[64,2,1024]{2,1,0:T(2,128)(2,1)S(1)}, u32[]{:S(2)}, u32[]{:S(2)}) async-start(bf16[64,2,1024]{2,1,0:T(2,128)(2,1)} %bitcast.4), calls=%async_computation.1 | async-start | bytes 524288 | tf_op jit(solution)/shard_map/all_to_all | solution.py:160
  30.9 1.0 copy-start.1
  34.1 12.3 %collective-permute-start.1 = (bf16[4,16,1024]{2,1,0:T(8,128)(2,1)S(1)}, bf16[4,16,1024]{2,1,0:T(8,128)(2,1)S(1)}, u32[]{:S(2)}, u32[]{:S(2)}) collective-permute-start(bf16[4,16,1024]{2,1,0:T(8,128)(2,1)S(1)} %get-tuple-element.21), channel_id=1, source_target_pairs={{0,64},{64,0},{1,65},{65,1},{2,66},{66,2},{3,67},{67,3},{4,68},{68... | collective-permute-start | bytes 393224 | tf_op jit(solution)/shard_map/ppermute | solution.py:139
  49.1 15.5 %all-to-all-start.2 = ((bf16[32,80,128]{2,1,0:T(8,128)(2,1)}), bf16[32,80,128]{2,1,0:T(8,128)(2,1)S(1)}, u32[]{:S(2)}, u32[]{:S(2)}) async-start(bf16[32,80,128]{2,1,0:T(8,128)(2,1)} %shard_map.86), calls=%async_computation.2 | async-start | bytes 1310720 | tf_op jit(solution)/shard_map/all_to_all | solution.py:204
  65.5 20.2 %all-to-all-start.3 = ((bf16[16,72,128]{2,1,0:T(8,128)(2,1)}), bf16[16,72,128]{2,1,0:T(8,128)(2,1)S(1)}, u32[]{:S(2)}, u32[]{:S(2)}) async-start(bf16[16,72,128]{2,1,0:T(8,128)(2,1)} %pad_maximum_fusion), calls=%async_computation.3 | async-start | bytes 589824 | tf_op jit(solution)/shard_map/all_to_all | solution.py:216
  86.5 16.0 %all-to-all-start.4 = ((bf16[32,48,128]{2,1,0:T(8,128)(2,1)}), bf16[32,48,128]{2,1,0:T(8,128)(2,1)S(1)}, u32[]{:S(2)}, u32[]{:S(2)}) async-start(bf16[32,48,128]{2,1,0:T(8,128)(2,1)} %get-tuple-element.30), calls=%async_computation.4 | async-start | bytes 786432 | tf_op jit(solution)/shard_map/all_to_all | solution.py:230

commit v4 on v3

--- a/solution.py
+++ b/solution.py
@@ -74,8 +74,13 @@
 
 
 def main_kernel(
-    l_ref, r_ref, m_ref, s_ref, g_ref, bias_ref, send_ref, o_ref, w_ref, left_ref
+    l_ref, r_ref, m_ref, s_ref, g_ref, rkeep_ref, rtake_ref, bias_ref, send_ref, rsum_ref, o_ref, w_ref, left_ref
 ):
+    for zq in range(4):
+        total = rkeep_ref[zq].astype(F32) + rtake_ref[zq].astype(F32)
+        for yh in range(4):
+            rows = [total[yh * 4 : yh * 4 + 4, t * K : (t + 1) * K] for t in range(8)]
+            rsum_ref[zq * 4 + yh] = jnp.concatenate(rows, axis=0).astype(BF16)
     right = r_ref[...] * jnp.concatenate([m_ref[...]] * C, axis=1)
     o_ref[...] = dot(l_ref[...], right, 0, 0).astype(BF16)
     pairs = s_ref[...]
@@ -104,18 +109,24 @@
                     ]
 
 
-def join_kernel(got_ref, l_ref, ml_ref, send_ref, left_ref, bias_ref):
+def join_kernel(got_ref, send_ref, bias_ref, total_ref):
     total = got_ref[0].astype(F32)
     for source in range(1, 16):
         total = total + got_ref[source].astype(F32)
     bias_ref[...] = total[64:65] + total[65:66]
-    rows = total[:64].astype(BF16)
-    for zb in range(2):
-        for core in range(2):
+    rows = total[32:64].astype(BF16)
+    total_ref[...] = total[:32]
+    for core in range(2):
+        right = [total_ref[pl.ds(core * 2 + q, 8, stride=4), :] for q in range(2)]
+        right = jnp.concatenate(right, axis=0).astype(BF16)
+        for zb in range(2):
             for col in range(8):
                 to = zb * 16 + core * 8 + col
-                send_ref[to, :32, :] = rows[32:64]
-                send_ref[to, 32:48, :] = rows[core * 16 : (core + 1) * 16]
+                send_ref[to, :32, :] = rows
+                send_ref[to, 32:48, :] = right
+
+
+def left_kernel(l_ref, ml_ref, left_ref):
     lane = lax.broadcasted_iota(jnp.int32, (8, 8 * C), 1) // C
     spread = (lane == lax.broadcasted_iota(jnp.int32, (8, 8 * C), 0)).astype(BF16)
     left = jnp.concatenate([l_ref[:16, :], l_ref[16:, :]], axis=1)
@@ -184,14 +195,14 @@
     )(
         at, keep, take, mask_i.astype(BF16), mask_i.T.astype(F32), mask_j.T.astype(F32), weight, left_all
     )
-    right_take = turn(right_give, "zb", 1)
-    right_take, right_all = lax.optimization_barrier((right_take, right_all))
-    right_part = (right_keep.astype(F32) + right_take.astype(F32)).astype(BF16)
-    send = pl.pallas_call(
+    send, right_part = pl.pallas_call(
         main_kernel,
-        out_shape=jax.ShapeDtypeStruct((32, 80, K), BF16),
-        in_specs=[VMEM] * 6,
-        out_specs=VMEM,
+        out_shape=(
+            jax.ShapeDtypeStruct((32, 80, K), BF16),
+            jax.ShapeDtypeStruct((16, 32, K), BF16),
+        ),
+        in_specs=[VMEM] * 8,
+        out_specs=(VMEM,) * 2,
         scratch_shapes=[
             pltpu.VMEM((TI * C, C * TJ), BF16),
             pltpu.VMEM((C * C, K), F32),
@@ -199,7 +210,7 @@
         ],
         compiler_params=pltpu.CompilerParams(vmem_limit_bytes=32 << 20),
         cost_estimate=pl.CostEstimate(flops=450_000_000, bytes_accessed=3_000_000, transcendentals=0),
-    )(left_all, right_all, mask_j.astype(BF16), scaled, grad, bias)
+    )(left_all, right_all, mask_j.astype(BF16), scaled, grad, right_keep, turn(right_give, "zb", 1), bias)
 
     got = lax.all_to_all(send, NEAR, 0, 0, tiled=True)
     total = jnp.sum(got[:, 32:72].astype(F32), axis=0)
@@ -208,23 +219,31 @@
     left_mask = lax.dynamic_slice(mask, (col_at * 16, row_at * 8), (16, 8)).astype(BF16)
     bias_sum = total[32] + total[33]
     high = lax.reduce_precision(bias_sum, 8, 7)
-    bias_rows = jnp.concatenate([high[None], (bias_sum - high)[None], jnp.zeros((6, K), F32)])
+    row = lax.broadcasted_iota(jnp.int32, (8, K), 0)
+    bias_rows = jnp.where(row == 0, high[None], jnp.where(row == 1, (bias_sum - high)[None], 0.0))
     rows = jnp.concatenate([total[:32], bias_rows]).astype(BF16)
     send = jnp.concatenate(
-        [right_part.reshape(16, 32, K), jnp.broadcast_to(rows[None], (16, 40, K))], axis=1
+        [right_part, jnp.broadcast_to(rows[None], (16, 40, K))], axis=1
     )
     got = lax.all_to_all(send, FAR, 0, 0, tiled=True)
-    send, left_grad, bias_sum = pl.pallas_call(
+    send, bias_sum = pl.pallas_call(
         join_kernel,
         out_shape=(
             jax.ShapeDtypeStruct((32, 48, K), BF16),
-            jax.ShapeDtypeStruct((16, 8 * C), BF16),
             jax.ShapeDtypeStruct((1, K), F32),
         ),
-        in_specs=[VMEM] * 3,
-        out_specs=(VMEM,) * 3,
-        compiler_params=pltpu.CompilerParams(vmem_limit_bytes=16 << 20),
-    )(got, left_sum, left_mask)
+        in_specs=[VMEM],
+        out_specs=(VMEM,) * 2,
+        scratch_shapes=[pltpu.VMEM((32, K), F32)],
+        compiler_params=pltpu.CompilerParams(vmem_limit_bytes=16 << 20),
+    )(got)
+    left_grad = pl.pallas_call(
+        left_kernel,
+        out_shape=jax.ShapeDtypeStruct((16, 8 * C), BF16),
+        in_specs=[VMEM] * 2,
+        out_specs=VMEM,
+        compiler_params=pltpu.CompilerParams(vmem_limit_bytes=16 << 20),
+    )(left_sum, left_mask)
     left_grad = left_grad.reshape(16, 8, C)
     bias_sum = bias_sum.reshape(K)
     got = lax.all_to_all(send, NEAR, 0, 0, tiled=True)

time: 104 us -> 103 us (level)
  blocking collectives: 0 us -> 20 us
  waiting for transfers between devices: 44.5 us -> 31.1 us
  starting transfers between devices: 45 us -> 38.2 us
    all_to_all x0 -> x1, blocking collectives: none -> 20 us  [per_device(): got = lax.all_to_all(send, FAR, 0, 0, tiled=True)]
    all_to_all x1 -> x0, waiting for transfers between devices: 13.3 us -> none  [per_device(): got = lax.all_to_all(send, FAR, 0, 0, tiled=True)]
    all_to_all x1 -> x0, starting transfers between devices: 6.76 us -> none  [per_device(): got = lax.all_to_all(send, FAR, 0, 0, tiled=True)]
    pallas_call x1 -> x2, Pallas kernels: 2.67 us -> 2.8 us  [the longest x1 2.67 us: per_device(): pl.pallas_call(main_kernel, out_shape=(jax.ShapeDtypeStruct((32, 80, K),...]
  transfers between devices with their start and end apart: 7 -> 6, of which waited for: 5 -> 4; matrix products, arithmetic and copies ran while one was open for 3% -> 3% of each run, Pallas kernels for 2% -> 2%
where the time goes in v4:
time: 103 us; the launch traced here: 102 us
  starting transfers between devices  38.2 us (37%)
  waiting for transfers between devices  31.1 us (30%)
  blocking collectives  20 us (19%)
  Pallas kernels  7.3 us (7%)
  local copies, waits for them, and re-layouts  4.42 us (4%)
    all_to_all x1, blocking collectives, per_device(): got = lax.all_to_all(send, FAR, 0, 0, tiled=True)  20 us
    all_to_all x2, waiting for transfers between devices, per_device(): got = lax.all_to_all(send, NEAR, 0, 0, tiled=True)  19.9 us
    all_to_all x1, starting transfers between devices, per_device(): right_all = lax.all_to_all(send, ROW, 0, 0, tiled=True).reshape(S, C * TJ)  12.1 us
    all_to_all x2, starting transfers between devices, per_device(): got = lax.all_to_all(send, NEAR, 0, 0, tiled=True)  10.5 us
    all_to_all x1, starting transfers between devices, per_device(): left_all = lax.all_to_all(send, ('core',) + COL, 0, 0, tiled=True)  10.2 us
    all_to_all x1, waiting for transfers between devices, per_device(): right_all = lax.all_to_all(send, ROW, 0, 0, tiled=True).reshape(S, C * TJ)  8.92 us
    ppermute x2, starting transfers between devices, turn(): return lax.ppermute(x, axis, [(i, (i + by) % n) for i in range(n)])  5.38 us
    pallas_call x1, Pallas kernels, per_device(): pl.pallas_call(main_kernel, out_shape=(jax.ShapeDtypeStruct((32, 80, K),...  2.67 us
  transfers between devices with their start and end apart: 6, of which 4 were waited for; matrix products, arithmetic and copies ran while one was open for 3% of the time, Pallas kernels for 2%

profile of v4, /device:TPU:1, one launch (start us, length us, event | category | flops | bytes accessed | tf_op | source)
XLA Modules:
  0.0 102.4 jit_solution(6142614486094959914)
XLA Ops:
  0.6 0.7 copy-done
  1.4 0.8 shard_map.84
  2.2 10.2 %all-to-all-start = ((bf16[16,16,256]{2,1,0:T(8,128)(2,1)}), bf16[16,16,256]{2,1,0:T(8,128)(2,1)S(1)}, u32[]{:S(2)}, u32[]{:S(2)}) async-start(bf16[16,16,256]{2,1,0:T(8,128)(2,1)} %shard_map.84), calls=%async_computation | async-start | bytes 262144 | tf_op jit(solution)/shard_map/all_to_all | solution.py:166
  12.4 0.7 copy-done.4
  13.3 0.8 broadcast_in_dim.36
  14.2 2.1 %collective-permute-start = (bf16[8,32,128]{2,1,0:T(8,128)(2,1)S(1)}, bf16[8,32,128]{2,1,0:T(8,128)(2,1)S(1)}, u32[]{:S(2)}, u32[]{:S(2)}) collective-permute-start(bf16[8,32,128]{2,1,0:T(8,128)(2,1)S(1)} %get-tuple-element.34), channel_id=1, source_target_pairs={{0,8},{8,0},{1,9},{9,1},{2,10},{10,2},{3,11},{11,3},{4,12},{12,4},... | collective-permute-start | bytes 196616 | tf_op jit(solution)/shard_map/ppermute | solution.py:150
  16.4 2.3 %all-to-all-done.l_in = bf16[16,16,256]{2,1,0:T(8,128)(2,1)S(1)} async-done(((bf16[16,16,256]{2,1,0:T(8,128)(2,1)}), bf16[16,16,256]{2,1,0:T(8,128)(2,1)S(1)}, u32[]{:S(2)}, u32[]{:S(2)}) %all-to-all-start) | async-done | bytes 131104 | tf_op jit(solution)/shard_map/all_to_all | solution.py:166
  18.7 12.1 %all-to-all-start.1 = ((bf16[64,2,1024]{2,1,0:T(2,128)(2,1)}), bf16[64,2,1024]{2,1,0:T(2,128)(2,1)S(1)}, u32[]{:S(2)}, u32[]{:S(2)}) async-start(bf16[64,2,1024]{2,1,0:T(2,128)(2,1)} %bitcast.4), calls=%async_computation.1 | async-start | bytes 524288 | tf_op jit(solution)/shard_map/all_to_all | solution.py:171
  31.1 0.1 copy.16.m_ref
  31.3 0.6 copy-done.1
  31.8 0.1 copy.15
  32.0 2.1 %shard_map.85 = (bf16[512,128]{1,0:T(8,128)(2,1)S(1)}, bf16[16,128]{1,0:T(8,128)(2,1)S(1)}, bf16[512,1024]{1,0:T(8,128)(2,1)S(1)}, bf16[128,512]{1,0:T(8,128)(2,...) custom-call(s32[2]{0:T(128)S(1)} %pad_add_fusion.at_ref, ...), custom_call_target="tpu_custom_call" | custom-call | flops 300000000 | bytes 3000000 | tf_op jit(solution)/shard_map/pallas_call | solution.py:180
  34.1 3.3 %collective-permute-start.1 = (bf16[4,16,1024]{2,1,0:T(8,128)(2,1)S(1)}, bf16[4,16,1024]{2,1,0:T(8,128)(2,1)S(1)}, u32[]{:S(2)}, u32[]{:S(2)}) collective-permute-start(bf16[4,16,1024]{2,1,0:T(8,128)(2,1)S(1)} %get-tuple-element.24), channel_id=1, source_target_pairs={{0,64},{64,0},{1,65},{65,1},{2,66},{66,2},{3,67},{67,3},{4,68},{68... | collective-permute-start | bytes 393224 | tf_op jit(solution)/shard_map/ppermute | solution.py:150
  37.4 8.9 %all-to-all-done.1 = bf16[64,2,1024]{2,1,0:T(2,128)(2,1)S(1)} async-done(((bf16[64,2,1024]{2,1,0:T(2,128)(2,1)}), bf16[64,2,1024]{2,1,0:T(2,128)(2,1)S(1)}, u32[]{:S(2)}, u32[]{:S(2)}) %all-to-all-start.1) | async-done | bytes 262176 | tf_op jit(solution)/shard_map/all_to_all | solution.py:171
  46.5 2.7 %shard_map.86 = (bf16[32,80,128]{2,1,0:T(8,128)(2,1)}, bf16[16,32,128]{2,1,0:T(8,128)(2,1)S(1)}) custom-call(bf16[128,512]{1,0:T(8,128)(2,1)S(1)} %get-tuple-element.19.l_ref, bf16[128,1024]{1,0:T(8,128)(2,1)S(1)} %reshape.81.r_ref, bf16[128,32]{1,0:T(8,128)(2,1)S(1)} %get-tuple-element.32.m_ref, bf16[512,128]{1,0:T(8,128)(2,1)S(1)} %get-tuple-element.21.s_ref, ...), custom_call_target="tpu_custom_call" | custom-call | flops 450000000 | bytes 3000000 | tf_op jit(solution)/shard_map/pallas_call | solution.py:198
  49.1 3.9 %all-to-all-start.2 = ((bf16[32,80,128]{2,1,0:T(8,128)(2,1)}), bf16[32,80,128]{2,1,0:T(8,128)(2,1)S(1)}, u32[]{:S(2)}, u32[]{:S(2)}) async-start(bf16[32,80,128]{2,1,0:T(8,128)(2,1)} %get-tuple-element.26), calls=%async_computation.2 | async-start | bytes 1310720 | tf_op jit(solution)/shard_map/all_to_all | solution.py:215
  53.1 11.5 %all-to-all-done.2 = bf16[32,80,128]{2,1,0:T(8,128)(2,1)S(1)} async-done(((bf16[32,80,128]{2,1,0:T(8,128)(2,1)}), bf16[32,80,128]{2,1,0:T(8,128)(2,1)S(1)}, u32[]{:S(2)}, u32[]{:S(2)}) %all-to-all-start.2) | async-done | bytes 655392 | tf_op jit(solution)/shard_map/all_to_all | solution.py:215
  64.8 20.0 %all_to_all.25.got_ref = bf16[16,72,128]{2,1,0:T(8,128)(2,1)S(1)} all-to-all(bf16[16,72,128]{2,1,0:T(8,128)(2,1)S(1)} %pad_maximum_fusion), channel_id=1, replica_groups=mesh['zq'=4,'zb'=2,'yh'=4,'core'=2,'yl'=2,'x'=4] {'zq','yh'}, dimensions={0} | all-to-all | bytes 589824 | tf_op jit(solution)/shard_map/all_to_all | solution.py:228
  84.8 0.8 shard_map.88
  85.6 6.6 %all-to-all-start.4 = ((bf16[32,48,128]{2,1,0:T(8,128)(2,1)}), bf16[32,48,128]{2,1,0:T(8,128)(2,1)S(1)}, u32[]{:S(2)}, u32[]{:S(2)}) async-start(bf16[32,48,128]{2,1,0:T(8,128)(2,1)} %get-tuple-element.28), calls=%async_computation.4 | async-start | bytes 786432 | tf_op jit(solution)/shard_map/all_to_all | solution.py:249
  92.4 0.1 shard_map.87
  92.5 0.7 reshape.82
  93.3 8.3 %all-to-all-done.4.got_ref = bf16[32,48,128]{2,1,0:T(8,128)(2,1)S(1)} async-done(((bf16[32,48,128]{2,1,0:T(8,128)(2,1)}), bf16[32,48,128]{2,1,0:T(8,128)(2,1)S(1)}, u32[]{:S(2)}, u32[]{:S(2)}) %all-to-all-start.4) | async-done | bytes 393248 | tf_op jit(solution)/shard_map/all_to_all | solution.py:249
  101.6 0.8 shard_map.89
  (31 shorter events, 1.1 us)
Async XLA Ops:
  0.6 0.8 copy-start
  2.2 16.6 %all-to-all-start = ((bf16[16,16,256]{2,1,0:T(8,128)(2,1)}), bf16[16,16,256]{2,1,0:T(8,128)(2,1)S(1)}, u32[]{:S(2)}, u32[]{:S(2)}) async-start(bf16[16,16,256]{2,1,0:T(8,128)(2,1)} %shard_map.84), calls=%async_computation | async-start | bytes 262144 | tf_op jit(solution)/shard_map/all_to_all | solution.py:166
  12.4 0.7 copy-start.4
  13.3 0.9 copy-start.2
  13.3 3.0 %copy-start.3 = (s32[128,512]{1,0:T(8,128)S(1)}, s32[128,512]{1,0:T(8,128)}, u32[]{:S(2)}) copy-start(s32[128,512]{1,0:T(8,128)} %param.9) | copy-start | bytes 786436
  14.2 17.8 %collective-permute-start = (bf16[8,32,128]{2,1,0:T(8,128)(2,1)S(1)}, bf16[8,32,128]{2,1,0:T(8,128)(2,1)S(1)}, u32[]{:S(2)}, u32[]{:S(2)}) collective-permute-start(bf16[8,32,128]{2,1,0:T(8,128)(2,1)S(1)} %get-tuple-element.34), channel_id=1, source_target_pairs={{0,8},{8,0},{1,9},{9,1},{2,10},{10,2},{3,11},{11,3},{4,12},{12,4},... | collective-permute-start | bytes 196616 | tf_op jit(solution)/shard_map/ppermute | solution.py:150
  18.7 27.6 %all-to-all-start.1 = ((bf16[64,2,1024]{2,1,0:T(2,128)(2,1)}), bf16[64,2,1024]{2,1,0:T(2,128)(2,1)S(1)}, u32[]{:S(2)}, u32[]{:S(2)}) async-start(bf16[64,2,1024]{2,1,0:T(2,128)(2,1)} %bitcast.4), calls=%async_computation.1 | async-start | bytes 524288 | tf_op jit(solution)/shard_map/all_to_all | solution.py:171
  30.9 1.0 copy-start.1
  34.1 12.3 %collective-permute-start.1 = (bf16[4,16,1024]{2,1,0:T(8,128)(2,1)S(1)}, bf16[4,16,1024]{2,1,0:T(8,128)(2,1)S(1)}, u32[]{:S(2)}, u32[]{:S(2)}) collective-permute-start(bf16[4,16,1024]{2,1,0:T(8,128)(2,1)S(1)} %get-tuple-element.24), channel_id=1, source_target_pairs={{0,64},{64,0},{1,65},{65,1},{2,66},{66,2},{3,67},{67,3},{4,68},{68... | collective-permute-start | bytes 393224 | tf_op jit(solution)/shard_map/ppermute | solution.py:150
  49.1 15.5 %all-to-all-start.2 = ((bf16[32,80,128]{2,1,0:T(8,128)(2,1)}), bf16[32,80,128]{2,1,0:T(8,128)(2,1)S(1)}, u32[]{:S(2)}, u32[]{:S(2)}) async-start(bf16[32,80,128]{2,1,0:T(8,128)(2,1)} %get-tuple-element.26), calls=%async_computation.2 | async-start | bytes 1310720 | tf_op jit(solution)/shard_map/all_to_all | solution.py:215
  85.6 16.0 %all-to-all-start.4 = ((bf16[32,48,128]{2,1,0:T(8,128)(2,1)}), bf16[32,48,128]{2,1,0:T(8,128)(2,1)S(1)}, u32[]{:S(2)}, u32[]{:S(2)}) async-start(bf16[32,48,128]{2,1,0:T(8,128)(2,1)} %get-tuple-element.28), calls=%async_computation.4 | async-start | bytes 786432 | tf_op jit(solution)/shard_map/all_to_all | solution.py:249

commit v5 on v4

--- a/solution.py
+++ b/solution.py
@@ -31,6 +31,17 @@
     left = jnp.concatenate([left[:, i, :] for i in range(8)], axis=1).astype(BF16)
     for to in range(16):
         send_ref[to] = left
+
+
+def turn_blocks(rows):
+    half = [jnp.concatenate([rows[a][:, :64], rows[a + 2][:, :64]], axis=1) for a in range(2)]
+    half += [jnp.concatenate([rows[a][:, 64:], rows[a + 2][:, 64:]], axis=1) for a in range(2)]
+    turned = []
+    for a, b in ((half[0], half[1]), (half[2], half[3])):
+        for at in (0, 32):
+            pieces = [x[:, y : y + 32] for y in (at, 64 + at) for x in (a, b)]
+            turned.append(jnp.concatenate(pieces, axis=1))
+    return turned
 
 
 def scale_kernel(
@@ -85,15 +96,12 @@
     o_ref[...] = dot(l_ref[...], right, 0, 0).astype(BF16)
     pairs = s_ref[...]
     for g in range(C // 4):
-        rows = []
-        for e in range(4):
-            at = g * K + e * TJ
-            rows.append(
-                jnp.concatenate(
-                    [o_ref[i * C : (i + 1) * C, at : at + TJ] for i in range(TI)], axis=1
-                )
-            )
-        outer = jnp.concatenate(rows, axis=0)
+        turned = [
+            turn_blocks([o_ref[i * C : (i + 1) * C, g * K : (g + 1) * K] for i in range(b, b + 4)])
+            for b in range(0, TI, 4)
+        ]
+        outer = [jnp.concatenate([blocks[e] for blocks in turned], axis=1) for e in range(4)]
+        outer = jnp.concatenate(outer, axis=0)
         w_ref[g * 4 * C : (g + 1) * 4 * C, :] = dot(outer, pairs, 1, 0)
     for c in range(C):
         send_ref[c, 32:64, :] = w_ref[pl.ds(c, C, stride=C), :].astype(BF16)
@@ -113,7 +121,7 @@
     total = got_ref[0].astype(F32)
     for source in range(1, 16):
         total = total + got_ref[source].astype(F32)
-    bias_ref[...] = total[64:65] + total[65:66]
+    bias_ref[...] = jnp.sum(total[64:], axis=0, keepdims=True)
     rows = total[32:64].astype(BF16)
     total_ref[...] = total[:32]
     for core in range(2):
@@ -217,13 +225,10 @@
     left_got = lax.dynamic_slice_in_dim(got, zb_at * 16, 16, 0)[:, :32]
     left_sum = jnp.sum(left_got.astype(F32), axis=0)
     left_mask = lax.dynamic_slice(mask, (col_at * 16, row_at * 8), (16, 8)).astype(BF16)
-    bias_sum = total[32] + total[33]
-    high = lax.reduce_precision(bias_sum, 8, 7)
-    row = lax.broadcasted_iota(jnp.int32, (8, K), 0)
-    bias_rows = jnp.where(row == 0, high[None], jnp.where(row == 1, (bias_sum - high)[None], 0.0))
-    rows = jnp.concatenate([total[:32], bias_rows]).astype(BF16)
+    high = lax.reduce_precision(total[32:], 8, 7)
+    rows = jnp.concatenate([total[:32], high, total[32:] - high]).astype(BF16)
     send = jnp.concatenate(
-        [right_part, jnp.broadcast_to(rows[None], (16, 40, K))], axis=1
+        [right_part, jnp.broadcast_to(rows[None], (16, 48, K))], axis=1
     )
     got = lax.all_to_all(send, FAR, 0, 0, tiled=True)
     send, bias_sum = pl.pallas_call(

time: 103 us -> 102 us (level)
  blocking collectives: 20 us -> 35.3 us
  waiting for transfers between devices: 31.1 us -> 19.6 us
  starting transfers between devices: 38.2 us -> 34.5 us
  Pallas kernels: 7.3 us -> 6.27 us
    all_to_all x0 -> x1, blocking collectives: none -> 14.8 us  [per_device(): got = lax.all_to_all(send, NEAR, 0, 0, tiled=True)]
    all_to_all x2 -> x1, waiting for transfers between devices: 19.9 us -> 8.34 us  [per_device(): got = lax.all_to_all(send, NEAR, 0, 0, tiled=True)]
    all_to_all x2 -> x1, starting transfers between devices: 10.5 us -> 6.79 us  [per_device(): got = lax.all_to_all(send, NEAR, 0, 0, tiled=True)]
  transfers between devices with their start and end apart: 6 -> 5, of which waited for: 4 -> 3; matrix products, arithmetic and copies ran while one was open for 3% -> 3% of each run, Pallas kernels for 2% -> 2%
where the time goes in v5:
time: 102 us; the launch traced here: 101 us
  blocking collectives  35.3 us (35%)
  starting transfers between devices  34.5 us (34%)
  waiting for transfers between devices  19.6 us (19%)
  Pallas kernels  6.27 us (6%)
  local copies, waits for them, and re-layouts  4.43 us (4%)
    all_to_all x1, blocking collectives, per_device(): got = lax.all_to_all(send, FAR, 0, 0, tiled=True)  20.5 us
    all_to_all x1, blocking collectives, per_device(): got = lax.all_to_all(send, NEAR, 0, 0, tiled=True)  14.8 us
    all_to_all x1, starting transfers between devices, per_device(): right_all = lax.all_to_all(send, ROW, 0, 0, tiled=True).reshape(S, C * TJ)  12.1 us
    all_to_all x1, starting transfers between devices, per_device(): left_all = lax.all_to_all(send, ('core',) + COL, 0, 0, tiled=True)  10.2 us
    all_to_all x1, waiting for transfers between devices, per_device(): right_all = lax.all_to_all(send, ROW, 0, 0, tiled=True).reshape(S, C * TJ)  8.92 us
    all_to_all x1, waiting for transfers between devices, per_device(): got = lax.all_to_all(send, NEAR, 0, 0, tiled=True)  8.34 us
    all_to_all x1, starting transfers between devices, per_device(): got = lax.all_to_all(send, NEAR, 0, 0, tiled=True)  6.79 us
    ppermute x2, starting transfers between devices, turn(): return lax.ppermute(x, axis, [(i, (i + by) % n) for i in range(n)])  5.38 us
  transfers between devices with their start and end apart: 5, of which 3 were waited for; matrix products, arithmetic and copies ran while one was open for 3% of the time, Pallas kernels for 2%

profile of v5, /device:TPU:1, one launch (start us, length us, event | category | flops | bytes accessed | tf_op | source)
XLA Modules:
  0.0 101.4 jit_solution(7353915370356565532)
XLA Ops:
  0.6 0.7 copy-done
  1.4 0.8 shard_map.84
  2.2 10.2 %all-to-all-start = ((bf16[16,16,256]{2,1,0:T(8,128)(2,1)}), bf16[16,16,256]{2,1,0:T(8,128)(2,1)S(1)}, u32[]{:S(2)}, u32[]{:S(2)}) async-start(bf16[16,16,256]{2,1,0:T(8,128)(2,1)} %shard_map.84), calls=%async_computation | async-start | bytes 262144 | tf_op jit(solution)/shard_map/all_to_all | solution.py:174
  12.4 0.7 copy-done.4
  13.2 0.1 broadcast_in_dim.6
  13.3 0.8 broadcast_in_dim.14
  14.2 2.1 %collective-permute-start = (bf16[8,32,128]{2,1,0:T(8,128)(2,1)S(1)}, bf16[8,32,128]{2,1,0:T(8,128)(2,1)S(1)}, u32[]{:S(2)}, u32[]{:S(2)}) collective-permute-start(bf16[8,32,128]{2,1,0:T(8,128)(2,1)S(1)} %get-tuple-element.34), channel_id=1, source_target_pairs={{0,8},{8,0},{1,9},{9,1},{2,10},{10,2},{3,11},{11,3},{4,12},{12,4},... | collective-permute-start | bytes 196616 | tf_op jit(solution)/shard_map/ppermute | solution.py:158
  16.4 2.3 %all-to-all-done.l_in = bf16[16,16,256]{2,1,0:T(8,128)(2,1)S(1)} async-done(((bf16[16,16,256]{2,1,0:T(8,128)(2,1)}), bf16[16,16,256]{2,1,0:T(8,128)(2,1)S(1)}, u32[]{:S(2)}, u32[]{:S(2)}) %all-to-all-start) | async-done | bytes 131104 | tf_op jit(solution)/shard_map/all_to_all | solution.py:174
  18.7 12.1 %all-to-all-start.1 = ((bf16[64,2,1024]{2,1,0:T(2,128)(2,1)}), bf16[64,2,1024]{2,1,0:T(2,128)(2,1)S(1)}, u32[]{:S(2)}, u32[]{:S(2)}) async-start(bf16[64,2,1024]{2,1,0:T(2,128)(2,1)} %bitcast.4), calls=%async_computation.1 | async-start | bytes 524288 | tf_op jit(solution)/shard_map/all_to_all | solution.py:179
  31.1 0.1 copy.16.m_ref
  31.3 0.6 copy-done.1
  31.8 0.1 copy.15
  32.0 2.1 %shard_map.85 = (bf16[512,128]{1,0:T(8,128)(2,1)S(1)}, bf16[16,128]{1,0:T(8,128)(2,1)S(1)}, bf16[512,1024]{1,0:T(8,128)(2,1)S(1)}, bf16[128,512]{1,0:T(8,128)(2,...) custom-call(s32[2]{0:T(128)S(1)} %pad_add_fusion.at_ref, ...), custom_call_target="tpu_custom_call" | custom-call | flops 300000000 | bytes 3000000 | tf_op jit(solution)/shard_map/pallas_call | solution.py:188
  34.1 3.3 %collective-permute-start.1 = (bf16[4,16,1024]{2,1,0:T(8,128)(2,1)S(1)}, bf16[4,16,1024]{2,1,0:T(8,128)(2,1)S(1)}, u32[]{:S(2)}, u32[]{:S(2)}) collective-permute-start(bf16[4,16,1024]{2,1,0:T(8,128)(2,1)S(1)} %get-tuple-element.24), channel_id=1, source_target_pairs={{0,64},{64,0},{1,65},{65,1},{2,66},{66,2},{3,67},{67,3},{4,68},{68... | collective-permute-start | bytes 393224 | tf_op jit(solution)/shard_map/ppermute | solution.py:158
  37.4 8.9 %all-to-all-done.1 = bf16[64,2,1024]{2,1,0:T(2,128)(2,1)S(1)} async-done(((bf16[64,2,1024]{2,1,0:T(2,128)(2,1)}), bf16[64,2,1024]{2,1,0:T(2,128)(2,1)S(1)}, u32[]{:S(2)}, u32[]{:S(2)}) %all-to-all-start.1) | async-done | bytes 262176 | tf_op jit(solution)/shard_map/all_to_all | solution.py:179
  46.4 1.6 %shard_map.86 = (bf16[32,80,128]{2,1,0:T(8,128)(2,1)S(1)}, bf16[16,32,128]{2,1,0:T(8,128)(2,1)S(1)}) custom-call(bf16[128,512]{1,0:T(8,128)(2,1)S(1)} %get-tuple-element.19.l_ref, bf16[128,1024]{1,0:T(8,128)(2,1)S(1)} %reshape.60.r_ref, bf16[128,32]{1,0:T(8,128)(2,1)S(1)} %get-tuple-element.32.m_ref, bf16[512,128]{1,0:T(8,128)(2,1)S(1)} %get-tuple-element.21.s_ref, ...), custom_call_target="tpu_custom_call" | custom-call | flops 450000000 | bytes 3000000 | tf_op jit(solution)/shard_map/pallas_call | solution.py:206
  48.1 14.8 %all_to_all.25 = bf16[32,80,128]{2,1,0:T(8,128)(2,1)S(1)} all-to-all(bf16[32,80,128]{2,1,0:T(8,128)(2,1)S(1)} %get-tuple-element.26), channel_id=1, replica_groups=mesh['zq'=4,'zb'=2,'yh'=4,'core'=2,'yl'=2,'x'=4] {'zb','core','yl','x'}, dimensions={0} | all-to-all | bytes 1310720 | tf_op jit(solution)/shard_map/all_to_all | solution.py:223
  63.1 20.5 %all_to_all.26.got_ref = bf16[16,80,128]{2,1,0:T(8,128)(2,1)S(1)} all-to-all(bf16[16,80,128]{2,1,0:T(8,128)(2,1)S(1)} %pad_maximum_fusion), channel_id=1, replica_groups=mesh['zq'=4,'zb'=2,'yh'=4,'core'=2,'yl'=2,'x'=4] {'zq','yh'}, dimensions={0} | all-to-all | bytes 655360 | tf_op jit(solution)/shard_map/all_to_all | solution.py:233
  83.6 0.8 shard_map.88
  84.4 6.8 %all-to-all-start.4 = ((bf16[32,48,128]{2,1,0:T(8,128)(2,1)}), bf16[32,48,128]{2,1,0:T(8,128)(2,1)S(1)}, u32[]{:S(2)}, u32[]{:S(2)}) async-start(bf16[32,48,128]{2,1,0:T(8,128)(2,1)} %get-tuple-element.28), calls=%async_computation.4 | async-start | bytes 786432 | tf_op jit(solution)/shard_map/all_to_all | solution.py:254
  91.4 0.1 shard_map.87
  91.5 0.7 reshape.61
  92.2 8.3 %all-to-all-done.4.got_ref = bf16[32,48,128]{2,1,0:T(8,128)(2,1)S(1)} async-done(((bf16[32,48,128]{2,1,0:T(8,128)(2,1)}), bf16[32,48,128]{2,1,0:T(8,128)(2,1)S(1)}, u32[]{:S(2)}, u32[]{:S(2)}) %all-to-all-start.4) | async-done | bytes 393248 | tf_op jit(solution)/shard_map/all_to_all | solution.py:254
  100.6 0.8 shard_map.89
  (28 shorter events, 1.0 us)
Async XLA Ops:
  0.6 0.8 copy-start
  2.2 16.6 %all-to-all-start = ((bf16[16,16,256]{2,1,0:T(8,128)(2,1)}), bf16[16,16,256]{2,1,0:T(8,128)(2,1)S(1)}, u32[]{:S(2)}, u32[]{:S(2)}) async-start(bf16[16,16,256]{2,1,0:T(8,128)(2,1)} %shard_map.84), calls=%async_computation | async-start | bytes 262144 | tf_op jit(solution)/shard_map/all_to_all | solution.py:174
  12.4 0.7 copy-start.4
  13.3 0.9 copy-start.2
  13.3 3.0 %copy-start.3 = (s32[128,512]{1,0:T(8,128)S(1)}, s32[128,512]{1,0:T(8,128)}, u32[]{:S(2)}) copy-start(s32[128,512]{1,0:T(8,128)} %param.9) | copy-start | bytes 786436
  14.2 17.8 %collective-permute-start = (bf16[8,32,128]{2,1,0:T(8,128)(2,1)S(1)}, bf16[8,32,128]{2,1,0:T(8,128)(2,1)S(1)}, u32[]{:S(2)}, u32[]{:S(2)}) collective-permute-start(bf16[8,32,128]{2,1,0:T(8,128)(2,1)S(1)} %get-tuple-element.34), channel_id=1, source_target_pairs={{0,8},{8,0},{1,9},{9,1},{2,10},{10,2},{3,11},{11,3},{4,12},{12,4},... | collective-permute-start | bytes 196616 | tf_op jit(solution)/shard_map/ppermute | solution.py:158
  18.7 27.6 %all-to-all-start.1 = ((bf16[64,2,1024]{2,1,0:T(2,128)(2,1)}), bf16[64,2,1024]{2,1,0:T(2,128)(2,1)S(1)}, u32[]{:S(2)}, u32[]{:S(2)}) async-start(bf16[64,2,1024]{2,1,0:T(2,128)(2,1)} %bitcast.4), calls=%async_computation.1 | async-start | bytes 524288 | tf_op jit(solution)/shard_map/all_to_all | solution.py:179
  30.9 1.0 copy-start.1
  34.1 12.3 %collective-permute-start.1 = (bf16[4,16,1024]{2,1,0:T(8,128)(2,1)S(1)}, bf16[4,16,1024]{2,1,0:T(8,128)(2,1)S(1)}, u32[]{:S(2)}, u32[]{:S(2)}) collective-permute-start(bf16[4,16,1024]{2,1,0:T(8,128)(2,1)S(1)} %get-tuple-element.24), channel_id=1, source_target_pairs={{0,64},{64,0},{1,65},{65,1},{2,66},{66,2},{3,67},{67,3},{4,68},{68... | collective-permute-start | bytes 393224 | tf_op jit(solution)/shard_map/ppermute | solution.py:158
  84.4 16.2 %all-to-all-start.4 = ((bf16[32,48,128]{2,1,0:T(8,128)(2,1)}), bf16[32,48,128]{2,1,0:T(8,128)(2,1)S(1)}, u32[]{:S(2)}, u32[]{:S(2)}) async-start(bf16[32,48,128]{2,1,0:T(8,128)(2,1)} %get-tuple-element.28), calls=%async_computation.4 | async-start | bytes 786432 | tf_op jit(solution)/shard_map/all_to_all | solution.py:254

commit v6 on v5

--- a/solution.py
+++ b/solution.py
@@ -85,7 +85,7 @@
 
 
 def main_kernel(
-    l_ref, r_ref, m_ref, s_ref, g_ref, rkeep_ref, rtake_ref, bias_ref, send_ref, rsum_ref, o_ref, w_ref, left_ref
+    l_ref, r_ref, m_ref, s_ref, g_ref, rkeep_ref, rtake_ref, bias_ref, send_ref, rsum_ref, o_ref, w_ref
 ):
     for zq in range(4):
         total = rkeep_ref[zq].astype(F32) + rtake_ref[zq].astype(F32)
@@ -106,15 +106,14 @@
     for c in range(C):
         send_ref[c, 32:64, :] = w_ref[pl.ds(c, C, stride=C), :].astype(BF16)
         send_ref[c, 64:80, :] = bias_ref[...]
-    left_ref[...] = dot(right, g_ref[...], 1, 1).astype(BF16)
+    left = dot(right, g_ref[...], 1, 1).astype(BF16)
     for zb in range(2):
         for core in range(2):
             for col in range(8):
                 for h in range(2):
                     at = core * 8 * C + h * K
-                    send_ref[zb * 16 + core * 8 + col, h * 16 : (h + 1) * 16, :] = left_ref[
-                        col * 16 : (col + 1) * 16, at : at + K
-                    ]
+                    rows = left[col * 16 : (col + 1) * 16, at : at + K]
+                    send_ref[zb * 16 + core * 8 + col, h * 16 : (h + 1) * 16, :] = rows
 
 
 def join_kernel(got_ref, send_ref, bias_ref, total_ref):
@@ -214,7 +213,6 @@
         scratch_shapes=[
             pltpu.VMEM((TI * C, C * TJ), BF16),
             pltpu.VMEM((C * C, K), F32),
-            pltpu.VMEM((S, TI * C), BF16),
         ],
         compiler_params=pltpu.CompilerParams(vmem_limit_bytes=32 << 20),
         cost_estimate=pl.CostEstimate(flops=450_000_000, bytes_accessed=3_000_000, transcendentals=0),

time: 102 us -> 102 us (level)
  no operation moved by 1% of the time
where the time goes in v6:
time: 102 us; the launch traced here: 101 us
  blocking collectives  35.3 us (35%)
  starting transfers between devices  34.5 us (34%)
  waiting for transfers between devices  19.6 us (19%)
  Pallas kernels  6.25 us (6%)
  local copies, waits for them, and re-layouts  4.43 us (4%)
    all_to_all x1, blocking collectives, per_device(): got = lax.all_to_all(send, FAR, 0, 0, tiled=True)  20.5 us
    all_to_all x1, blocking collectives, per_device(): got = lax.all_to_all(send, NEAR, 0, 0, tiled=True)  14.8 us
    all_to_all x1, starting transfers between devices, per_device(): right_all = lax.all_to_all(send, ROW, 0, 0, tiled=True).reshape(S, C * TJ)  12.1 us
    all_to_all x1, starting transfers between devices, per_device(): left_all = lax.all_to_all(send, ('core',) + COL, 0, 0, tiled=True)  10.2 us
    all_to_all x1, waiting for transfers between devices, per_device(): right_all = lax.all_to_all(send, ROW, 0, 0, tiled=True).reshape(S, C * TJ)  8.92 us
    all_to_all x1, waiting for transfers between devices, per_device(): got = lax.all_to_all(send, NEAR, 0, 0, tiled=True)  8.34 us
    all_to_all x1, starting transfers between devices, per_device(): got = lax.all_to_all(send, NEAR, 0, 0, tiled=True)  6.79 us
    ppermute x2, starting transfers between devices, turn(): return lax.ppermute(x, axis, [(i, (i + by) % n) for i in range(n)])  5.38 us
  transfers between devices with their start and end apart: 5, of which 3 were waited for; matrix products, arithmetic and copies ran while one was open for 3% of the time, Pallas kernels for 2%

profile of v6, /device:TPU:1, one launch (start us, length us, event | category | flops | bytes accessed | tf_op | source)
XLA Modules:
  0.0 101.4 jit_solution(17211449650067852031)
XLA Ops:
  0.6 0.7 copy-done
  1.4 0.8 shard_map.84
  2.2 10.2 %all-to-all-start = ((bf16[16,16,256]{2,1,0:T(8,128)(2,1)}), bf16[16,16,256]{2,1,0:T(8,128)(2,1)S(1)}, u32[]{:S(2)}, u32[]{:S(2)}) async-start(bf16[16,16,256]{2,1,0:T(8,128)(2,1)} %shard_map.84), calls=%async_computation | async-start | bytes 262144 | tf_op jit(solution)/shard_map/all_to_all | solution.py:173
  12.4 0.7 copy-done.4
  13.2 0.1 broadcast_in_dim.6
  13.3 0.8 broadcast_in_dim.14
  14.2 2.1 %collective-permute-start = (bf16[8,32,128]{2,1,0:T(8,128)(2,1)S(1)}, bf16[8,32,128]{2,1,0:T(8,128)(2,1)S(1)}, u32[]{:S(2)}, u32[]{:S(2)}) collective-permute-start(bf16[8,32,128]{2,1,0:T(8,128)(2,1)S(1)} %get-tuple-element.34), channel_id=1, source_target_pairs={{0,8},{8,0},{1,9},{9,1},{2,10},{10,2},{3,11},{11,3},{4,12},{12,4},... | collective-permute-start | bytes 196616 | tf_op jit(solution)/shard_map/ppermute | solution.py:157
  16.4 2.3 %all-to-all-done.l_in = bf16[16,16,256]{2,1,0:T(8,128)(2,1)S(1)} async-done(((bf16[16,16,256]{2,1,0:T(8,128)(2,1)}), bf16[16,16,256]{2,1,0:T(8,128)(2,1)S(1)}, u32[]{:S(2)}, u32[]{:S(2)}) %all-to-all-start) | async-done | bytes 131104 | tf_op jit(solution)/shard_map/all_to_all | solution.py:173
  18.7 12.1 %all-to-all-start.1 = ((bf16[64,2,1024]{2,1,0:T(2,128)(2,1)}), bf16[64,2,1024]{2,1,0:T(2,128)(2,1)S(1)}, u32[]{:S(2)}, u32[]{:S(2)}) async-start(bf16[64,2,1024]{2,1,0:T(2,128)(2,1)} %bitcast.4), calls=%async_computation.1 | async-start | bytes 524288 | tf_op jit(solution)/shard_map/all_to_all | solution.py:178
  31.1 0.1 copy.16.m_ref
  31.3 0.6 copy-done.1
  31.8 0.1 copy.15
  32.0 2.1 %shard_map.85 = (bf16[512,128]{1,0:T(8,128)(2,1)S(1)}, bf16[16,128]{1,0:T(8,128)(2,1)S(1)}, bf16[512,1024]{1,0:T(8,128)(2,1)S(1)}, bf16[128,512]{1,0:T(8,128)(2,...) custom-call(s32[2]{0:T(128)S(1)} %pad_add_fusion.at_ref, ...), custom_call_target="tpu_custom_call" | custom-call | flops 300000000 | bytes 3000000 | tf_op jit(solution)/shard_map/pallas_call | solution.py:187
  34.1 3.3 %collective-permute-start.1 = (bf16[4,16,1024]{2,1,0:T(8,128)(2,1)S(1)}, bf16[4,16,1024]{2,1,0:T(8,128)(2,1)S(1)}, u32[]{:S(2)}, u32[]{:S(2)}) collective-permute-start(bf16[4,16,1024]{2,1,0:T(8,128)(2,1)S(1)} %get-tuple-element.24), channel_id=1, source_target_pairs={{0,64},{64,0},{1,65},{65,1},{2,66},{66,2},{3,67},{67,3},{4,68},{68... | collective-permute-start | bytes 393224 | tf_op jit(solution)/shard_map/ppermute | solution.py:157
  37.4 8.9 %all-to-all-done.1 = bf16[64,2,1024]{2,1,0:T(2,128)(2,1)S(1)} async-done(((bf16[64,2,1024]{2,1,0:T(2,128)(2,1)}), bf16[64,2,1024]{2,1,0:T(2,128)(2,1)S(1)}, u32[]{:S(2)}, u32[]{:S(2)}) %all-to-all-start.1) | async-done | bytes 262176 | tf_op jit(solution)/shard_map/all_to_all | solution.py:178
  46.4 1.6 %shard_map.86 = (bf16[32,80,128]{2,1,0:T(8,128)(2,1)S(1)}, bf16[16,32,128]{2,1,0:T(8,128)(2,1)S(1)}) custom-call(bf16[128,512]{1,0:T(8,128)(2,1)S(1)} %get-tuple-element.19.l_ref, bf16[128,1024]{1,0:T(8,128)(2,1)S(1)} %reshape.60.r_ref, bf16[128,32]{1,0:T(8,128)(2,1)S(1)} %get-tuple-element.32.m_ref, bf16[512,128]{1,0:T(8,128)(2,1)S(1)} %get-tuple-element.21.s_ref, ...), custom_call_target="tpu_custom_call" | custom-call | flops 450000000 | bytes 3000000 | tf_op jit(solution)/shard_map/pallas_call | solution.py:205
  48.1 14.8 %all_to_all.25 = bf16[32,80,128]{2,1,0:T(8,128)(2,1)S(1)} all-to-all(bf16[32,80,128]{2,1,0:T(8,128)(2,1)S(1)} %get-tuple-element.26), channel_id=1, replica_groups=mesh['zq'=4,'zb'=2,'yh'=4,'core'=2,'yl'=2,'x'=4] {'zb','core','yl','x'}, dimensions={0} | all-to-all | bytes 1310720 | tf_op jit(solution)/shard_map/all_to_all | solution.py:221
  63.1 20.5 %all_to_all.26.got_ref = bf16[16,80,128]{2,1,0:T(8,128)(2,1)S(1)} all-to-all(bf16[16,80,128]{2,1,0:T(8,128)(2,1)S(1)} %pad_maximum_fusion), channel_id=1, replica_groups=mesh['zq'=4,'zb'=2,'yh'=4,'core'=2,'yl'=2,'x'=4] {'zq','yh'}, dimensions={0} | all-to-all | bytes 655360 | tf_op jit(solution)/shard_map/all_to_all | solution.py:231
  83.6 0.8 shard_map.88
  84.4 6.8 %all-to-all-start.4 = ((bf16[32,48,128]{2,1,0:T(8,128)(2,1)}), bf16[32,48,128]{2,1,0:T(8,128)(2,1)S(1)}, u32[]{:S(2)}, u32[]{:S(2)}) async-start(bf16[32,48,128]{2,1,0:T(8,128)(2,1)} %get-tuple-element.28), calls=%async_computation.4 | async-start | bytes 786432 | tf_op jit(solution)/shard_map/all_to_all | solution.py:252
  91.4 0.1 shard_map.87
  91.5 0.7 reshape.61
  92.2 8.3 %all-to-all-done.4.got_ref = bf16[32,48,128]{2,1,0:T(8,128)(2,1)S(1)} async-done(((bf16[32,48,128]{2,1,0:T(8,128)(2,1)}), bf16[32,48,128]{2,1,0:T(8,128)(2,1)S(1)}, u32[]{:S(2)}, u32[]{:S(2)}) %all-to-all-start.4) | async-done | bytes 393248 | tf_op jit(solution)/shard_map/all_to_all | solution.py:252
  100.6 0.8 shard_map.89
  (28 shorter events, 1.0 us)
Async XLA Ops:
  0.6 0.8 copy-start
  2.2 16.6 %all-to-all-start = ((bf16[16,16,256]{2,1,0:T(8,128)(2,1)}), bf16[16,16,256]{2,1,0:T(8,128)(2,1)S(1)}, u32[]{:S(2)}, u32[]{:S(2)}) async-start(bf16[16,16,256]{2,1,0:T(8,128)(2,1)} %shard_map.84), calls=%async_computation | async-start | bytes 262144 | tf_op jit(solution)/shard_map/all_to_all | solution.py:173
  12.4 0.7 copy-start.4
  13.3 0.9 copy-start.2
  13.3 3.0 %copy-start.3 = (s32[128,512]{1,0:T(8,128)S(1)}, s32[128,512]{1,0:T(8,128)}, u32[]{:S(2)}) copy-start(s32[128,512]{1,0:T(8,128)} %param.9) | copy-start | bytes 786436
  14.2 17.8 %collective-permute-start = (bf16[8,32,128]{2,1,0:T(8,128)(2,1)S(1)}, bf16[8,32,128]{2,1,0:T(8,128)(2,1)S(1)}, u32[]{:S(2)}, u32[]{:S(2)}) collective-permute-start(bf16[8,32,128]{2,1,0:T(8,128)(2,1)S(1)} %get-tuple-element.34), channel_id=1, source_target_pairs={{0,8},{8,0},{1,9},{9,1},{2,10},{10,2},{3,11},{11,3},{4,12},{12,4},... | collective-permute-start | bytes 196616 | tf_op jit(solution)/shard_map/ppermute | solution.py:157
  18.7 27.6 %all-to-all-start.1 = ((bf16[64,2,1024]{2,1,0:T(2,128)(2,1)}), bf16[64,2,1024]{2,1,0:T(2,128)(2,1)S(1)}, u32[]{:S(2)}, u32[]{:S(2)}) async-start(bf16[64,2,1024]{2,1,0:T(2,128)(2,1)} %bitcast.4), calls=%async_computation.1 | async-start | bytes 524288 | tf_op jit(solution)/shard_map/all_to_all | solution.py:178
  30.9 1.0 copy-start.1
  34.1 12.3 %collective-permute-start.1 = (bf16[4,16,1024]{2,1,0:T(8,128)(2,1)S(1)}, bf16[4,16,1024]{2,1,0:T(8,128)(2,1)S(1)}, u32[]{:S(2)}, u32[]{:S(2)}) collective-permute-start(bf16[4,16,1024]{2,1,0:T(8,128)(2,1)S(1)} %get-tuple-element.24), channel_id=1, source_target_pairs={{0,64},{64,0},{1,65},{65,1},{2,66},{66,2},{3,67},{67,3},{4,68},{68... | collective-permute-start | bytes 393224 | tf_op jit(solution)/shard_map/ppermute | solution.py:157
  84.4 16.2 %all-to-all-start.4 = ((bf16[32,48,128]{2,1,0:T(8,128)(2,1)}), bf16[32,48,128]{2,1,0:T(8,128)(2,1)S(1)}, u32[]{:S(2)}, u32[]{:S(2)}) async-start(bf16[32,48,128]{2,1,0:T(8,128)(2,1)} %get-tuple-element.28), calls=%async_computation.4 | async-start | bytes 786432 | tf_op jit(solution)/shard_map/all_to_all | solution.py:252
